TPU v7x, 256 devices: a whole 4x4x8 slice. The times are simulated.
256 devices in a mesh: lib: 32 (over z, x_lo, core), ref: 8 (over y, x_hi).
Axes of the slice: x: 4 (x_hi: 2, x_lo: 2; x = x_hi * 2 + x_lo), y: 4, z: 8, core: 2. Of those that a mesh axis runs over, the one named last changes fastest.
Arguments:
- compounds: bfloat16 [262144, 512], P(('lib', 'ref')), may hold values from 0 to 2.5, as said below
- compound_weight: float32 [262144], P(('lib', 'ref')), may hold values from 0.5 to 12, as said below
- reference_prints: bfloat16 [4096, 512], P('ref'), may hold values from 0 to 2.5, as said below
- potency: bfloat16 [4096], P('ref'), may hold values from 4 to 10
- target_label: int32 [4096], P('ref'), may hold values from 0 to 255, as said below
Outputs:
- whitened: float32 [262144, 256], P(('lib', 'ref'))
Inputs may be any that keep to these rules, and one draw needn't show every extreme that they name: `target_label`: each of the 256 targets labels exactly 16 actives. `compounds`: nonnegative; every row has an entry of 0.25 or more. `reference_prints`: nonnegative; every row has an entry of 0.25 or more. `compound_weight`: positive.
All inputs are finite; a program needn't handle non-finite values.
Results may differ from a plain program's by a relative error of at most 0.0015.
Values may be sent and summed in bfloat16 or wider, within the bound.
No kernel may reach another device: no remote copies, remote signals or barrier semaphores. Data moves between devices by JAX's collectives and lax.ppermute only.
A program may use at most 64 MiB of HBM per device.

v0:
```python
import functools

import jax
import jax.numpy as jnp
from jax import lax
from jax.experimental import pallas as pl
from jax.experimental.pallas import tpu as pltpu
from jax.sharding import PartitionSpec as P

ALL = ("lib", "ref")
BITS = 512
EXTRA = 16
DEPTH = BITS + EXTRA
TARGETS = 256
SHRINKAGE = 0.02
LOG2E = 1.4426950408889634
SCALE = 320.0 * LOG2E
MARGIN = 58.0
PANEL = 32
REDO = 128
F32 = jnp.float32
BF16 = jnp.bfloat16
EXACT = lax.Precision.HIGHEST
VMEM = pl.BlockSpec(memory_space=pltpu.VMEM)


def params(mib=40):
    return pltpu.CompilerParams(vmem_limit_bytes=mib * 2**20)


def cost(flops, size):
    return pl.CostEstimate(flops=flops, bytes_accessed=size, transcendentals=0)


def place(x, y, z, c):
    return ((z % 8 * 2 + x % 2) * 2 + c % 2) * 8 + y % 4 * 2 + x // 2


def route(move):
    pairs = []
    for x in range(4):
        for y in range(4):
            for z in range(8):
                for c in range(2):
                    pairs.append((place(x, y, z, c), place(*move(x, y, z, c))))
    return sorted(pairs)


def send(value, move):
    return lax.ppermute(value, ALL, route(move))


def up(x, y, z, c):
    return x, y + 1, z, c


def down(x, y, z, c):
    return x, y - 1, z, c


def up2(x, y, z, c):
    return x, y + 2, z, c


def flip(x, y, z, c):
    return 3 - x, y, z, c


def sibling(x, y, z, c):
    return x, y, z, 1 - c


def prep_kernel(core_ref, prints_ref, potency_ref, label_ref, whole_ref, half_ref):
    prints = prints_ref[...].T
    wide = prints.astype(F32)
    norm = jnp.sum(wide * wide, axis=0, keepdims=True)
    high = norm.astype(BF16)
    rest = norm - high.astype(F32)
    middle = rest.astype(BF16)
    low = (rest - middle.astype(F32)).astype(BF16)
    row = lax.broadcasted_iota(jnp.int32, (EXTRA, prints.shape[1]), 0)
    extra = jnp.where(row == 0, potency_ref[...].astype(F32), 0.0)
    extra = jnp.where(row == 1, label_ref[...].astype(F32), extra)
    for at, part in ((2, high), (3, middle), (4, low)):
        extra = jnp.where(row == at, part.astype(F32), extra)
    extra = extra.astype(BF16)
    whole_ref[:BITS, :] = prints
    whole_ref[BITS:, :] = extra
    first = core_ref[0] == 0
    half = prints.shape[1] // 2

    @pl.when(first)
    def _():
        half_ref[:BITS, :] = prints[:, :half]
        half_ref[BITS:, :] = extra[:, :half]

    @pl.when(jnp.logical_not(first))
    def _():
        half_ref[:BITS, :] = prints[:, half:]
        half_ref[BITS:, :] = extra[:, half:]


def prepare(core, prints, potency, label):
    refs = prints.shape[0]
    return pl.pallas_call(
        prep_kernel,
        in_specs=[pl.BlockSpec(memory_space=pltpu.SMEM), VMEM, VMEM, VMEM],
        out_specs=[VMEM, VMEM],
        out_shape=[
            jax.ShapeDtypeStruct((DEPTH, refs), BF16),
            jax.ShapeDtypeStruct((DEPTH, refs // 2), BF16),
        ],
        compiler_params=params(),
        name="prepare",
    )(core, prints, potency, label)


def piece_scores(queries, query_norm, piece_ref):
    extra = piece_ref[BITS:, :].astype(F32)
    norm = extra[2:3] + extra[3:4] + extra[4:5]
    inter = jnp.dot(queries, piece_ref[:BITS, :], preferred_element_type=F32)
    inverse = 1.0 / ((query_norm + norm) - inter)
    return (inter * inverse) * SCALE


def piece_values(piece_ref):
    extra = piece_ref[BITS:, :].astype(F32)
    target = lax.broadcasted_iota(jnp.int32, (TARGETS, extra.shape[1]), 0)
    hit = target == extra[1:2].astype(jnp.int32)
    return jnp.where(hit, extra[0:1], 0.0).astype(BF16)


def add_piece(scores, top, piece_ref, num, den):
    expo = jnp.exp2(scores - top).astype(BF16)
    rounded = expo.astype(F32)
    for k in range(expo.shape[1] // 128):
        den = den + rounded[:, k * 128 : (k + 1) * 128]
    num = num + lax.dot_general(
        expo,
        piece_values(piece_ref),
        (((1,), (1,)), ((), ())),
        preferred_element_type=F32,
    )
    return num, den


def squared_norm(queries):
    wide = queries.astype(F32)
    return jnp.sum(wide * wide, axis=1, keepdims=True)


def first_kernel(queries_ref, piece_ref, num_ref, den_ref, top_ref):
    queries = queries_ref[...]
    rows = queries.shape[0]
    scores = piece_scores(queries, squared_norm(queries), piece_ref)
    top = jnp.max(scores, axis=1, keepdims=True) + MARGIN
    num = jnp.zeros((rows, TARGETS), F32)
    den = jnp.zeros((rows, 128), F32)
    num, den = add_piece(scores, top, piece_ref, num, den)
    num_ref[...] = num
    den_ref[...] = den
    top_ref[...] = jnp.broadcast_to(top, (rows, 128))


def more_kernel(count, *refs):
    queries_ref, num_in, den_in, top_ref = refs[:4]
    pieces = refs[4 : 4 + count]
    num_ref, den_ref = refs[4 + count :]
    queries = queries_ref[...]
    query_norm = squared_norm(queries)
    top = top_ref[:, 0:1]
    num, den = num_in[...], den_in[...]
    for piece_ref in pieces:
        scores = piece_scores(queries, query_norm, piece_ref)
        num, den = add_piece(scores, top, piece_ref, num, den)
    num_ref[...] = num
    den_ref[...] = den


def last_kernel(count, past, *refs):
    queries_ref, num_in, den_in, top_ref, weight_ref = refs[:5]
    pieces = refs[5 : 5 + count]
    earlier = refs[5 + count : 5 + count + past]
    profile_ref, moments_ref = refs[5 + count + past : 7 + count + past]
    buffer, done = refs[7 + count + past :]
    rows = queries_ref.shape[0]
    queries = queries_ref[...]
    query_norm = squared_norm(queries)
    top = top_ref[:, 0:1]
    num, den = num_in[...], den_in[...]
    for piece_ref in pieces:
        scores = piece_scores(queries, query_norm, piece_ref)
        num, den = add_piece(scores, top, piece_ref, num, den)
    total = jnp.sum(den, axis=1, keepdims=True)
    profile_ref[...] = num * (1.0 / total)

    @pl.when(jnp.logical_not(jnp.max(total) <= 1.0))
    def _():
        width = pieces[0].shape[1]
        sources = list(pieces)
        for source in earlier:
            sources += [source.at[:, pl.ds(k, width)] for k in range(0, source.shape[1], width)]
        copies = [
            pltpu.make_async_copy(source, buffer.at[k], done.at[k])
            for k, source in enumerate(sources)
        ]
        for copy in copies:
            copy.start()
        for copy in copies:
            copy.wait()

        @pl.loop(0, rows // REDO)
        def _(block):
            here = pl.ds(pl.multiple_of(block * REDO, REDO), REDO)
            queries = queries_ref[here, :]
            query_norm = squared_norm(queries)

            def highest(k, best):
                scores = piece_scores(queries, query_norm, buffer.at[k])
                return jnp.maximum(best, jnp.max(scores, axis=1, keepdims=True))

            def collect(k, sums):
                scores = piece_scores(queries, query_norm, buffer.at[k])
                return add_piece(scores, best, buffer.at[k], *sums)

            best = lax.fori_loop(0, len(sources), highest, jnp.full((REDO, 1), -1.0, F32))
            blank = jnp.zeros((REDO, TARGETS), F32), jnp.zeros((REDO, 128), F32)
            num, den = lax.fori_loop(0, len(sources), collect, blank)
            profile_ref[here, :] = num * (1.0 / jnp.sum(den, axis=1, keepdims=True))

    profile = profile_ref[...]
    weight = weight_ref[...]
    weight_total = jnp.sum(weight, axis=0, keepdims=True)
    first = jnp.sum(profile * weight, axis=0, keepdims=True)
    mean = first / weight_total
    spread = (profile - mean) * jnp.sqrt(weight)
    outer = (((0,), (0,)), ((), ()))
    moments = lax.dot_general(
        spread, spread, outer, precision=EXACT, preferred_element_type=F32
    ) + lax.dot_general(mean, first, outer, precision=EXACT, preferred_element_type=F32)
    row = lax.broadcasted_iota(jnp.int32, (TARGETS, TARGETS), 0)
    column = lax.broadcasted_iota(jnp.int32, (TARGETS, TARGETS), 1)
    moments = jnp.where((row == 0) & (column > 0), first, moments)
    moments = jnp.where((row == 1) & (column == 2), first[0:1, 0:1], moments)
    moments = jnp.where((row == 1) & (column == 3), weight_total, moments)
    moments_ref[...] = moments


def work(rows, pieces):
    refs = sum(piece.shape[1] for piece in pieces)
    return cost(6 * rows * refs * (BITS + TARGETS), rows * 2048 + refs * DEPTH * 2)


def first_part(queries, piece):
    rows = queries.shape[0]
    return pl.pallas_call(
        first_kernel,
        in_specs=[VMEM, VMEM],
        out_specs=[VMEM] * 3,
        out_shape=[
            jax.ShapeDtypeStruct((rows, TARGETS), F32),
            jax.ShapeDtypeStruct((rows, 128), F32),
            jax.ShapeDtypeStruct((rows, 128), F32),
        ],
        compiler_params=params(),
        cost_estimate=work(rows, [piece]),
        name="first_part",
    )(queries, piece)


def more_part(queries, state, pieces):
    rows = queries.shape[0]
    num, den = pl.pallas_call(
        functools.partial(more_kernel, len(pieces)),
        in_specs=[VMEM] * (4 + len(pieces)),
        out_specs=[VMEM] * 2,
        out_shape=[
            jax.ShapeDtypeStruct((rows, TARGETS), F32),
            jax.ShapeDtypeStruct((rows, 128), F32),
        ],
        compiler_params=params(),
        cost_estimate=work(rows, pieces),
        name="more_part",
    )(queries, *state, *pieces)
    return num, den, state[2]


def last_part(queries, state, weight, pieces, earlier):
    rows, width = queries.shape[0], pieces[0].shape[1]
    count = sum(piece.shape[1] // width for piece in [*pieces, *earlier])
    return pl.pallas_call(
        functools.partial(last_kernel, len(pieces), len(earlier)),
        in_specs=[VMEM] * (5 + len(pieces)) + [pl.BlockSpec(memory_space=pl.ANY)] * len(earlier),
        out_specs=[VMEM] * 2,
        out_shape=[
            jax.ShapeDtypeStruct((rows, TARGETS), F32),
            jax.ShapeDtypeStruct((TARGETS, TARGETS), F32),
        ],
        scratch_shapes=[pltpu.VMEM((count, DEPTH, width), BF16), pltpu.SemaphoreType.DMA((count,))],
        compiler_params=params(),
        cost_estimate=work(rows, pieces),
        name="last_part",
    )(queries, *state, weight, *pieces, *earlier)


def repeat_row(block, at):
    return jnp.broadcast_to(block[at : at + 1, :], block.shape)


def inverse_factor(schur, size):
    groups = PANEL // 8
    panels = size // PANEL
    sub = lax.broadcasted_iota(jnp.int32, (8, 128), 0)
    eye = (
        lax.broadcasted_iota(jnp.int32, (PANEL, PANEL), 0)
        == lax.broadcasted_iota(jnp.int32, (PANEL, PANEL), 1)
    ).astype(F32)
    schur = [schur[i * PANEL : (i + 1) * PANEL, :] for i in range(panels)]
    inverse = [None] * panels
    result = []
    for t in range(panels):
        start = t * PANEL
        lane0 = start // 128 * 128
        left = schur[t][:, lane0:]
        right = [inverse[t]] if t else []
        right.append(eye)
        width = start + PANEL
        if width % 128:
            right.append(jnp.zeros((PANEL, -width % 128), F32))
        right = jnp.concatenate(right, axis=1)
        nl, nr = left.shape[1] // 128, right.shape[1] // 128
        tiles = [
            [left[8 * g : 8 * g + 8, 128 * k : 128 * k + 128] for k in range(nl)]
            + [right[8 * g : 8 * g + 8, 128 * k : 128 * k + 128] for k in range(nr)]
            for g in range(groups)
        ]
        square = left[:, start - lane0 : start - lane0 + PANEL]
        spread = [
            [
                jnp.broadcast_to(square[8 * g : 8 * g + 8, k : k + 1], (8, 128))
                if g >= k // 8
                else None
                for g in range(groups)
            ]
            for k in range(PANEL)
        ]
        inverses = []
        for k in range(PANEL):
            own, at = divmod(k, 8)
            inv = 1.0 / repeat_row(spread[k][own], at)
            inverses.append(inv)
            column = [
                spread[k][g] if g > own else jnp.where(sub > at, spread[k][g], 0.0) if g == own else None
                for g in range(groups)
            ]
            for m in range(k + 1, PANEL):
                factor = repeat_row(spread[k][m // 8], m % 8)
                for g in range(m // 8, groups):
                    spread[m][g] = spread[m][g] - (column[g] * factor) * inv
            multiple = [None if c is None else c * inv for c in column]
            for k2 in range(nl + nr):
                row = repeat_row(tiles[own][k2], at)
                for g in range(own, groups):
                    tiles[g][k2] = tiles[g][k2] - multiple[g] * row
        scale = []
        for g in range(groups):
            column = inverses[8 * g]
            for o in range(1, 8):
                column = jnp.where(sub == o, inverses[8 * g + o], column)
            scale.append(column)
        root = [jnp.sqrt(column) for column in scale]
        blank = [jnp.zeros((8, 128), F32)] * (size // 128 - nr)
        result.append(
            jnp.concatenate(
                [
                    jnp.concatenate([tiles[g][nl + k] * root[g] for k in range(nr)] + blank, axis=1)
                    for g in range(groups)
                ],
                axis=0,
            )
        )
        if t == panels - 1:
            break
        upper = jnp.concatenate([jnp.concatenate(tiles[g], axis=1) for g in range(groups)], axis=0)
        scaled = jnp.concatenate(
            [
                jnp.concatenate([tiles[g][k] * scale[g] for k in range(nl)], axis=1)
                for g in range(groups)
            ],
            axis=0,
        )
        for low, high in ((t + 1, t + 2), (t + 2, panels)):
            if low >= high:
                continue
            update = lax.dot_general(
                scaled[:, low * PANEL - lane0 : high * PANEL - lane0],
                upper,
                (((0,), (0,)), ((), ())),
                precision=EXACT,
                preferred_element_type=F32,
            )
            for i in range(low, high):
                part = update[(i - low) * PANEL : (i - low + 1) * PANEL]
                kept = [schur[i][:, :lane0]] if lane0 else []
                schur[i] = jnp.concatenate(kept + [schur[i][:, lane0:] - part[:, : nl * 128]], axis=1)
                fresh = -part[:, nl * 128 : nl * 128 + width]
                if inverse[i] is not None:
                    fresh = jnp.concatenate([inverse[i] + fresh[:, :start], fresh[:, start:]], axis=1)
                inverse[i] = fresh
    return jnp.concatenate(result, axis=0)


def whiten_kernel(moments_ref, profile_ref, weight_ref, out_ref):
    total = moments_ref[...]
    row = lax.broadcasted_iota(jnp.int32, (TARGETS, TARGETS), 0)
    column = lax.broadcasted_iota(jnp.int32, (TARGETS, TARGETS), 1)
    share = 1.0 / total[1:2, 3:4]
    first = jnp.where(column[0:1] == 0, total[1:2, 2:3], total[0:1, :])
    mean = first * share
    outer = lax.dot_general(
        mean, mean, (((0,), (0,)), ((), ())), precision=EXACT, preferred_element_type=F32
    )
    lower = jnp.where(column <= row, total, 0.0)
    strict = jnp.where(column < row, total, 0.0)
    covariance = (lower + strict.T) * share - outer
    covariance = covariance + jnp.where(row == column, SHRINKAGE, 0.0)
    inverse = inverse_factor(covariance, TARGETS)
    centered = (profile_ref[...] - mean) * jnp.sqrt(weight_ref[...])
    out_ref[...] = lax.dot_general(
        centered, inverse, (((1,), (1,)), ((), ())), precision=EXACT, preferred_element_type=F32
    )


def whiten(moments, profile, weight):
    return pl.pallas_call(
        whiten_kernel,
        in_specs=[VMEM, VMEM, VMEM],
        out_specs=VMEM,
        out_shape=jax.ShapeDtypeStruct(profile.shape, F32),
        compiler_params=params(),
        name="whiten",
    )(moments, profile, weight)


def on_device(compounds, compound_weight, reference_prints, potency, target_label):
    devices = lax.axis_size(ALL)
    core = lax.rem(lax.axis_index("lib"), 2).astype(jnp.int32).reshape(1)
    weight = compound_weight[:, None]
    own, half = prepare(core, reference_prints, potency[None, :], target_label[None, :])

    hold = lax.optimization_barrier
    far, flipped = send(half, up2), send(half, flip)
    above, below = send(half, up), send(half, down)
    state = first_part(compounds, own)
    flipped, above, below, state = hold((flipped, above, below, state))
    flipped_above, flipped_below = send(flipped, up), send(flipped, down)
    others = [send(piece, sibling) for piece in (flipped, above, below)]
    state = more_part(compounds, state, [flipped, above, below])
    far, others, state = hold((far, others, state))
    flipped_far, other_far = send(far, flip), send(far, sibling)
    state = more_part(compounds, state, others + [far])
    flipped_above, flipped_below, other_far, state = hold(
        (flipped_above, flipped_below, other_far, state)
    )
    other_above, other_below = send(flipped_above, sibling), send(flipped_below, sibling)
    state = more_part(compounds, state, [other_far, flipped_above, flipped_below])
    other_flipped_far = send(flipped_far, sibling)
    later = [other_above, other_below, flipped_far, other_flipped_far]
    earlier = [own, flipped, above, below, *others, far, other_far, flipped_above, flipped_below]
    profile, moments = last_part(compounds, state, weight, later, earlier)

    shares = lax.all_to_all(moments.reshape(devices, 2, TARGETS // 2), ALL, 0, 0)
    share = jnp.sum(shares, axis=0, keepdims=True)
    total = lax.all_to_all(jnp.broadcast_to(share, shares.shape), ALL, 0, 0)
    return whiten(total.reshape(TARGETS, TARGETS), profile, weight)


def solution(mesh):
    placed = (P(("lib", "ref"), None), P(("lib", "ref")), P("ref", None), P("ref"), P("ref"))
    return jax.shard_map(
        on_device, mesh=mesh, in_specs=placed, out_specs=P(("lib", "ref"), None), check_vma=False
    )
```

profile of v0, /device:TPU:1, one launch (start us, length us, event | category | flops | bytes accessed | tf_op | source)
XLA Modules:
  0.0 188.2 jit_solution(10242837689510547561)
XLA Ops:
  0.0 0.7 copy-done.12
  0.7 0.7 copy-done.1
  1.4 1.0 copy-done
  2.4 0.9 prepare.1
  3.4 3.6 %collective-permute-start.2 = (bf16[528,256]{1,0:T(8,128)(2,1)}, bf16[528,256]{1,0:T(8,128)(2,1)S(1)}, u32[]{:S(2)}, u32[]{:S(2)}) collective-permute-start(bf16[528,256]{1,0:T(8,128)(2,1)} %get-tuple-element.37), channel_id=1, source_target_pairs={{0,6},{1,7},{2,0},{3,1},{4,2},{5,3},{6,4},{7,5},{8,14},{9,15},{10,... | collective-permute-start | bytes 811016 | tf_op jit(solution)/shard_map/ppermute | solution.py:50
  6.9 2.5 %collective-permute-start = (bf16[528,256]{1,0:T(8,128)(2,1)}, bf16[528,256]{1,0:T(8,128)(2,1)S(1)}, u32[]{:S(2)}, u32[]{:S(2)}) collective-permute-start(bf16[528,256]{1,0:T(8,128)(2,1)} %get-tuple-element.37), channel_id=1, source_target_pairs={{0,17},{1,16},{2,19},{3,18},{4,21},{5,20},{6,23},{7,22},{8,25},{9,... | collective-permute-start | bytes 811016 | tf_op jit(solution)/shard_map/ppermute | solution.py:50
  9.4 1.6 collective-permute-start.5
  11.0 0.2 copy.6.refs_4_.weight_ref
  11.3 1.9 %first_part.1 = (f32[1024,256]{1,0:T(8,128)S(1)}, f32[1024,128]{1,0:T(8,128)S(1)}, f32[1024,128]{1,0:T(8,128)S(1)}) custom-call(bf16[1024,512]{1,0:T(8,128)(2,1)S(1)} %copy-done.2, bf16[528,512]{1,0:T(8,128)(2,1)S(1)} %get-tuple-element.38.piece_ref.refs_9_), custom_call_target="tpu_custom_call" | custom-call | flops 2415919104 | bytes 2637824 | tf_op jit(solution)/shard_map/first_part/pallas_call | solution.py:256
  13.2 3.2 %collective-permute-done.1.refs_5_.refs_11_ = bf16[528,256]{1,0:T(8,128)(2,1)S(1)} collective-permute-done((bf16[528,256]{1,0:T(8,128)(2,1)}, bf16[528,256]{1,0:T(8,128)(2,1)S(1)}, u32[]{:S(2)}, u32[]{:S(2)}) %collective-permute-start.1) | collective-permute-done | bytes 270368 | tf_op jit(solution)/shard_map/ppermute | solution.py:50
  16.4 6.7 %collective-permute-start.6 = (bf16[528,256]{1,0:T(8,128)(2,1)S(1)}, bf16[528,256]{1,0:T(8,128)(2,1)S(1)}, u32[]{:S(2)}, u32[]{:S(2)}) collective-permute-start(bf16[528,256]{1,0:T(8,128)(2,1)S(1)} %collective-permute-done.refs_4_.refs_10_), channel_id=1, source_target_pairs={{0,8},{1,9},{2,10},{3,11},{4,12},{5,13},{6,14},{7,15},{8,0},{9,1},... | collective-permute-start | bytes 811016 | tf_op jit(solution)/shard_map/ppermute | solution.py:50
  23.1 0.0 collective-permute-start.4
  23.2 0.4 collective-permute-start.7
  23.5 0.2 collective-permute-start.8
  23.7 2.1 %more_part.3 = (f32[1024,256]{1,0:T(8,128)S(1)}, f32[1024,128]{1,0:T(8,128)S(1)}) custom-call(bf16[1024,512]{1,0:T(8,128)(2,1)S(1)} %copy-done.2, f32[1024,256]{1,0:T(8,128)S(1)} %get-tuple-element.45.refs_1_, f32[1024,128]{1,0:T(8,128)S(1)} %get-tuple-element.46.refs_2_, f32[1024,128]{1,0:T(8,128)S(1)} %get-tuple-element.61.refs_3_, ...), custom_call_target="tpu_custom_call" | custom-call | flops 3623878656 | bytes 2908160 | tf_op jit(solution)/shard_map/more_part/pallas_call | solution.py:273
  25.9 1.5 collective-permute-start.3
  27.4 2.6 %collective-permute-start.12 = (bf16[528,256]{1,0:T(8,128)(2,1)S(1)}, bf16[528,256]{1,0:T(8,128)(2,1)S(1)}, u32[]{:S(2)}, u32[]{:S(2)}) collective-permute-start(bf16[528,256]{1,0:T(8,128)(2,1)S(1)} %collective-permute-done.5.refs_7_.refs_16_), channel_id=1, source_target_pairs={{0,17},{1,16},{2,19},{3,18},{4,21},{5,20},{6,23},{7,22},{8,25},{9,... | collective-permute-start | bytes 811016 | tf_op jit(solution)/shard_map/ppermute | solution.py:50
  30.0 0.9 collective-permute-start.9
  30.9 2.4 %more_part.4 = (f32[1024,256]{1,0:T(8,128)S(1)}, f32[1024,128]{1,0:T(8,128)S(1)}) custom-call(bf16[1024,512]{1,0:T(8,128)(2,1)S(1)} %copy-done.2, f32[1024,256]{1,0:T(8,128)S(1)} %get-tuple-element.51.refs_1_, f32[1024,128]{1,0:T(8,128)S(1)} %get-tuple-element.52.refs_2_, f32[1024,128]{1,0:T(8,128)S(1)} %get-tuple-element.61.refs_3_, ...), custom_call_target="tpu_custom_call" | custom-call | flops 4831838208 | bytes 3178496 | tf_op jit(solution)/shard_map/more_part/pallas_call | solution.py:273
  33.3 1.5 collective-permute-done.3.refs_5_.refs_18_
  34.9 0.0 copy-start.10
  34.9 1.3 collective-permute-start.10
  36.2 0.1 collective-permute-start.11
  36.3 1.3 collective-permute-start.13
  37.6 2.1 %more_part.5 = (f32[1024,256]{1,0:T(8,128)S(1)}, f32[1024,128]{1,0:T(8,128)S(1)}) custom-call(bf16[1024,512]{1,0:T(8,128)(2,1)S(1)} %copy-done.2, f32[1024,256]{1,0:T(8,128)S(1)} %get-tuple-element.59.refs_1_, f32[1024,128]{1,0:T(8,128)S(1)} %get-tuple-element.60.refs_2_, f32[1024,128]{1,0:T(8,128)S(1)} %get-tuple-element.61.refs_3_, ...), custom_call_target="tpu_custom_call" | custom-call | flops 3623878656 | bytes 2908160 | tf_op jit(solution)/shard_map/more_part/pallas_call | solution.py:273
  39.8 88.6 %last_part.1 = (f32[1024,256]{1,0:T(8,128)S(1)}, f32[256,256]{1,0:T(8,128)S(1)}) custom-call(bf16[1024,512]{1,0:T(8,128)(2,1)S(1)} %copy-done.2, f32[1024,256]{1,0:T(8,128)S(1)} %get-tuple-element.65.refs_1_, f32[1024,128]{1,0:T(8,128)S(1)} %get-tuple-element.66.refs_2_, f32[1024,128]{1,0:T(8,128)S(1)} %get-tuple-element.61.refs_3_, ...), custom_call_target="tpu_custom_call" | custom-call | flops 4831838208 | bytes 3178496 | tf_op jit(solution)/shard_map/last_part/pallas_call | solution.py:291
  128.4 0.1 reshape.11
  128.5 27.9 %all_to_all.10 = f32[256,2,128]{2,1,0:T(2,128)S(1)} all-to-all(f32[256,2,128]{2,1,0:T(2,128)S(1)} %reshape.11), channel_id=1, replica_groups=mesh['lib'=32,'ref'=8] {'lib','ref'}, dimensions={0} | all-to-all | bytes 524288 | tf_op jit(solution)/shard_map/all_to_all | solution.py:472
  156.4 0.3 reduce_sum.9
  156.7 0.1 broadcast_in_dim.18
  156.8 20.6 %all_to_all.11 = f32[256,2,128]{2,1,0:T(2,128)S(1)} all-to-all(f32[256,2,128]{2,1,0:T(2,128)S(1)} %broadcast_in_dim.18), channel_id=1, replica_groups=mesh['lib'=32,'ref'=8] {'lib','ref'}, dimensions={0} | all-to-all | bytes 524288 | tf_op jit(solution)/shard_map/all_to_all | solution.py:474
  177.4 10.8 %whiten.1 = f32[1024,256]{1,0:T(8,128)} custom-call(f32[256,256]{1,0:T(8,128)S(1)} %bitcast.7, f32[1024,256]{1,0:T(8,128)S(1)} %get-tuple-element.68.profile_ref, f32[1024,1]{1,0:T(8,128)S(1)} %copy.6.refs_4_.weight_ref), custom_call_target="tpu_custom_call" | custom-call | tf_op jit(solution)/shard_map/whiten/pallas_call | solution.py:435
  (37 shorter events, 0.1 us)
Async XLA Ops:
  0.0 0.7 copy-start.12
  0.7 10.4 %copy-start.11 = (f32[1024]{0:T(1024)S(1)}, f32[1024]{0:T(1024)}, u32[]{:S(2)}) copy-start(f32[1024]{0:T(1024)} %param.6) | copy-start | bytes 12292
  0.7 0.7 copy-start.1
  1.4 1.0 copy-start
  2.4 8.9 %copy-start.2 = (bf16[1024,512]{1,0:T(8,128)(2,1)S(1)}, bf16[1024,512]{1,0:T(8,128)(2,1)}, u32[]{:S(2)}) copy-start(bf16[1024,512]{1,0:T(8,128)(2,1)} %refs_0_.7) | copy-start | bytes 3145732
  3.4 9.9 %collective-permute-start.2 = (bf16[528,256]{1,0:T(8,128)(2,1)}, bf16[528,256]{1,0:T(8,128)(2,1)S(1)}, u32[]{:S(2)}, u32[]{:S(2)}) collective-permute-start(bf16[528,256]{1,0:T(8,128)(2,1)} %get-tuple-element.37), channel_id=1, source_target_pairs={{0,6},{1,7},{2,0},{3,1},{4,2},{5,3},{6,4},{7,5},{8,14},{9,15},{10,... | collective-permute-start | bytes 811016 | tf_op jit(solution)/shard_map/ppermute | solution.py:50
  6.9 9.5 %collective-permute-start.1 = (bf16[528,256]{1,0:T(8,128)(2,1)}, bf16[528,256]{1,0:T(8,128)(2,1)S(1)}, u32[]{:S(2)}, u32[]{:S(2)}) collective-permute-start(bf16[528,256]{1,0:T(8,128)(2,1)} %get-tuple-element.37), channel_id=1, source_target_pairs={{0,2},{1,3},{2,4},{3,5},{4,6},{5,7},{6,0},{7,1},{8,10},{9,11},{10,... | collective-permute-start | bytes 811016 | tf_op jit(solution)/shard_map/ppermute | solution.py:50
  6.9 9.5 %collective-permute-start = (bf16[528,256]{1,0:T(8,128)(2,1)}, bf16[528,256]{1,0:T(8,128)(2,1)S(1)}, u32[]{:S(2)}, u32[]{:S(2)}) collective-permute-start(bf16[528,256]{1,0:T(8,128)(2,1)} %get-tuple-element.37), channel_id=1, source_target_pairs={{0,17},{1,16},{2,19},{3,18},{4,21},{5,20},{6,23},{7,22},{8,25},{9,... | collective-permute-start | bytes 811016 | tf_op jit(solution)/shard_map/ppermute | solution.py:50
  9.4 16.4 %collective-permute-start.5 = (bf16[528,256]{1,0:T(8,128)(2,1)}, bf16[528,256]{1,0:T(8,128)(2,1)S(1)}, u32[]{:S(2)}, u32[]{:S(2)}) collective-permute-start(bf16[528,256]{1,0:T(8,128)(2,1)} %get-tuple-element.37), channel_id=1, source_target_pairs={{0,4},{1,5},{2,6},{3,7},{4,0},{5,1},{6,2},{7,3},{8,12},{9,13},{10,... | collective-permute-start | bytes 811016 | tf_op jit(solution)/shard_map/ppermute | solution.py:50
  13.2 12.6 %copy-start.3 = (bf16[528,256]{1,0:T(8,128)(2,1)}, bf16[528,256]{1,0:T(8,128)(2,1)S(1)}, u32[]{:S(2)}) copy-start(bf16[528,256]{1,0:T(8,128)(2,1)S(1)} %collective-permute-done.2.refs_6_.refs_12_) | copy-start | bytes 811012
  16.4 9.4 %copy-start.5 = (bf16[528,256]{1,0:T(8,128)(2,1)}, bf16[528,256]{1,0:T(8,128)(2,1)S(1)}, u32[]{:S(2)}) copy-start(bf16[528,256]{1,0:T(8,128)(2,1)S(1)} %collective-permute-done.1.refs_5_.refs_11_) | copy-start | bytes 811012
  16.4 9.5 %copy-start.7 = (bf16[528,256]{1,0:T(8,128)(2,1)}, bf16[528,256]{1,0:T(8,128)(2,1)S(1)}, u32[]{:S(2)}) copy-start(bf16[528,256]{1,0:T(8,128)(2,1)S(1)} %collective-permute-done.refs_4_.refs_10_) | copy-start | bytes 811012
  16.4 11.0 %collective-permute-start.6 = (bf16[528,256]{1,0:T(8,128)(2,1)S(1)}, bf16[528,256]{1,0:T(8,128)(2,1)S(1)}, u32[]{:S(2)}, u32[]{:S(2)}) collective-permute-start(bf16[528,256]{1,0:T(8,128)(2,1)S(1)} %collective-permute-done.refs_4_.refs_10_), channel_id=1, source_target_pairs={{0,8},{1,9},{2,10},{3,11},{4,12},{5,13},{6,14},{7,15},{8,0},{9,1},... | collective-permute-start | bytes 811016 | tf_op jit(solution)/shard_map/ppermute | solution.py:50
  23.1 10.2 %collective-permute-start.4 = (bf16[528,256]{1,0:T(8,128)(2,1)S(1)}, bf16[528,256]{1,0:T(8,128)(2,1)S(1)}, u32[]{:S(2)}, u32[]{:S(2)}) collective-permute-start(bf16[528,256]{1,0:T(8,128)(2,1)S(1)} %collective-permute-done.refs_4_.refs_10_), channel_id=1, source_target_pairs={{0,6},{1,7},{2,0},{3,1},{4,2},{5,3},{6,4},{7,5},{8,14},{9,15},{10,... | collective-permute-start | bytes 811016 | tf_op jit(solution)/shard_map/ppermute | solution.py:50
  23.2 4.2 %collective-permute-start.7 = (bf16[528,256]{1,0:T(8,128)(2,1)S(1)}, bf16[528,256]{1,0:T(8,128)(2,1)S(1)}, u32[]{:S(2)}, u32[]{:S(2)}) collective-permute-start(bf16[528,256]{1,0:T(8,128)(2,1)S(1)} %collective-permute-done.1.refs_5_.refs_11_), channel_id=1, source_target_pairs={{0,8},{1,9},{2,10},{3,11},{4,12},{5,13},{6,14},{7,15},{8,0},{9,1},... | collective-permute-start | bytes 811016 | tf_op jit(solution)/shard_map/ppermute | solution.py:50
  23.5 3.9 %collective-permute-start.8 = (bf16[528,256]{1,0:T(8,128)(2,1)S(1)}, bf16[528,256]{1,0:T(8,128)(2,1)S(1)}, u32[]{:S(2)}, u32[]{:S(2)}) collective-permute-start(bf16[528,256]{1,0:T(8,128)(2,1)S(1)} %collective-permute-done.2.refs_6_.refs_12_), channel_id=1, source_target_pairs={{0,8},{1,9},{2,10},{3,11},{4,12},{5,13},{6,14},{7,15},{8,0},{9,1},... | collective-permute-start | bytes 811016 | tf_op jit(solution)/shard_map/ppermute | solution.py:50
  25.9 7.4 %copy-start.9 = (bf16[528,256]{1,0:T(8,128)(2,1)}, bf16[528,256]{1,0:T(8,128)(2,1)S(1)}, u32[]{:S(2)}) copy-start(bf16[528,256]{1,0:T(8,128)(2,1)S(1)} %collective-permute-done.5.refs_7_.refs_16_) | copy-start | bytes 811012
  25.9 9.0 %collective-permute-start.3 = (bf16[528,256]{1,0:T(8,128)(2,1)S(1)}, bf16[528,256]{1,0:T(8,128)(2,1)S(1)}, u32[]{:S(2)}, u32[]{:S(2)}) collective-permute-start(bf16[528,256]{1,0:T(8,128)(2,1)S(1)} %collective-permute-done.refs_4_.refs_10_), channel_id=1, source_target_pairs={{0,2},{1,3},{2,4},{3,5},{4,6},{5,7},{6,0},{7,1},{8,10},{9,11},{10,... | collective-permute-start | bytes 811016 | tf_op jit(solution)/shard_map/ppermute | solution.py:50
  27.4 8.9 %collective-permute-start.12 = (bf16[528,256]{1,0:T(8,128)(2,1)S(1)}, bf16[528,256]{1,0:T(8,128)(2,1)S(1)}, u32[]{:S(2)}, u32[]{:S(2)}) collective-permute-start(bf16[528,256]{1,0:T(8,128)(2,1)S(1)} %collective-permute-done.5.refs_7_.refs_16_), channel_id=1, source_target_pairs={{0,17},{1,16},{2,19},{3,18},{4,21},{5,20},{6,23},{7,22},{8,25},{9,... | collective-permute-start | bytes 811016 | tf_op jit(solution)/shard_map/ppermute | solution.py:50
  30.0 4.9 %collective-permute-start.9 = (bf16[528,256]{1,0:T(8,128)(2,1)S(1)}, bf16[528,256]{1,0:T(8,128)(2,1)S(1)}, u32[]{:S(2)}, u32[]{:S(2)}) collective-permute-start(bf16[528,256]{1,0:T(8,128)(2,1)S(1)} %collective-permute-done.5.refs_7_.refs_16_), channel_id=1, source_target_pairs={{0,8},{1,9},{2,10},{3,11},{4,12},{5,13},{6,14},{7,15},{8,0},{9,1},... | collective-permute-start | bytes 811016 | tf_op jit(solution)/shard_map/ppermute | solution.py:50
  34.9 4.9 %copy-start.4 = (bf16[528,256]{1,0:T(8,128)(2,1)S(1)}, bf16[528,256]{1,0:T(8,128)(2,1)}, u32[]{:S(2)}) copy-start(bf16[528,256]{1,0:T(8,128)(2,1)} %copy-done.3) | copy-start | bytes 811012
  34.9 4.9 %copy-start.6 = (bf16[528,256]{1,0:T(8,128)(2,1)S(1)}, bf16[528,256]{1,0:T(8,128)(2,1)}, u32[]{:S(2)}) copy-start(bf16[528,256]{1,0:T(8,128)(2,1)} %copy-done.5) | copy-start | bytes 811012
  34.9 4.9 %copy-start.8 = (bf16[528,256]{1,0:T(8,128)(2,1)S(1)}, bf16[528,256]{1,0:T(8,128)(2,1)}, u32[]{:S(2)}) copy-start(bf16[528,256]{1,0:T(8,128)(2,1)} %copy-done.7) | copy-start | bytes 811012
  34.9 4.9 %copy-start.10 = (bf16[528,256]{1,0:T(8,128)(2,1)S(1)}, bf16[528,256]{1,0:T(8,128)(2,1)}, u32[]{:S(2)}) copy-start(bf16[528,256]{1,0:T(8,128)(2,1)} %copy-done.9) | copy-start | bytes 811012
  34.9 4.9 %collective-permute-start.10 = (bf16[528,256]{1,0:T(8,128)(2,1)S(1)}, bf16[528,256]{1,0:T(8,128)(2,1)S(1)}, u32[]{:S(2)}, u32[]{:S(2)}) collective-permute-start(bf16[528,256]{1,0:T(8,128)(2,1)S(1)} %collective-permute-done.3.refs_5_.refs_18_), channel_id=1, source_target_pairs={{0,8},{1,9},{2,10},{3,11},{4,12},{5,13},{6,14},{7,15},{8,0},{9,1},... | collective-permute-start | bytes 811016 | tf_op jit(solution)/shard_map/ppermute | solution.py:50
  36.2 3.6 %collective-permute-start.11 = (bf16[528,256]{1,0:T(8,128)(2,1)S(1)}, bf16[528,256]{1,0:T(8,128)(2,1)S(1)}, u32[]{:S(2)}, u32[]{:S(2)}) collective-permute-start(bf16[528,256]{1,0:T(8,128)(2,1)S(1)} %collective-permute-done.4.refs_6_.refs_19_), channel_id=1, source_target_pairs={{0,8},{1,9},{2,10},{3,11},{4,12},{5,13},{6,14},{7,15},{8,0},{9,1},... | collective-permute-start | bytes 811016 | tf_op jit(solution)/shard_map/ppermute | solution.py:50
  36.3 3.5 %collective-permute-start.13 = (bf16[528,256]{1,0:T(8,128)(2,1)S(1)}, bf16[528,256]{1,0:T(8,128)(2,1)S(1)}, u32[]{:S(2)}, u32[]{:S(2)}) collective-permute-start(bf16[528,256]{1,0:T(8,128)(2,1)S(1)} %collective-permute-done.12.refs_7_), channel_id=1, source_target_pairs={{0,8},{1,9},{2,10},{3,11},{4,12},{5,13},{6,14},{7,15},{8,0},{9,1},... | collective-permute-start | bytes 811016 | tf_op jit(solution)/shard_map/ppermute | solution.py:50
where the time goes:
time: 188 us
  Pallas kernels  109 us (58%)
  blocking collectives  48.5 us (26%)
  starting transfers between devices  22.7 us (12%)
  waiting for transfers between devices  4.75 us (3%)
  local copies, waits for them, and re-layouts  2.9 us (2%)
    pallas_call x1, Pallas kernels, last_part(): pl.pallas_call(functools.partial(last_kernel, len(pieces), len(earlier)),...  88.6 us
    all_to_all x1, blocking collectives, on_device(): lax.all_to_all(moments.reshape(devices, 2, TARGETS // 2), ALL, 0, 0)  27.9 us
    ppermute x14, starting transfers between devices, send(): return lax.ppermute(value, ALL, route(move))  22.7 us
    all_to_all x1, blocking collectives, on_device(): total = lax.all_to_all(jnp.broadcast_to(share, shares.shape), ALL, 0, 0)  20.6 us
    pallas_call x1, Pallas kernels, whiten(): pl.pallas_call(whiten_kernel, in_specs=[VMEM, VMEM, VMEM], out_specs=VMEM...  10.8 us
    pallas_call x3, Pallas kernels, more_part(): pl.pallas_call(functools.partial(more_kernel, len(pieces)), in_specs=[VME...  6.7 us
    ppermute x14, waiting for transfers between devices, send(): return lax.ppermute(value, ALL, route(move))  4.75 us
  transfers between devices with their start and end apart: 14, of which 2 were waited for; matrix products, arithmetic and copies ran while one was open for 0% of the time, Pallas kernels for 5%

commit v1 on v0

--- a/solution.py
+++ b/solution.py
@@ -7,7 +7,8 @@
 from jax.experimental.pallas import tpu as pltpu
 from jax.sharding import PartitionSpec as P
 
-ALL = ("lib", "ref")
+ALL = ("z", "x_lo", "core", "y", "x_hi")
+PLANE = ("x_lo", "core", "y", "x_hi")
 BITS = 512
 EXTRA = 16
 DEPTH = BITS + EXTRA
@@ -24,7 +25,7 @@
 VMEM = pl.BlockSpec(memory_space=pltpu.VMEM)
 
 
-def params(mib=40):
+def params(mib=20):
     return pltpu.CompilerParams(vmem_limit_bytes=mib * 2**20)
 
 
@@ -58,19 +59,23 @@
     return x, y - 1, z, c
 
 
-def up2(x, y, z, c):
-    return x, y + 2, z, c
-
-
 def flip(x, y, z, c):
     return 3 - x, y, z, c
 
 
+def onward(x, y, z, c):
+    return x, y + 1 - 2 * c, z, c
+
+
+def across(x, y, z, c):
+    return 3 - x, y + 1 - 2 * c, z, c
+
+
 def sibling(x, y, z, c):
     return x, y, z, 1 - c
 
 
-def prep_kernel(core_ref, prints_ref, potency_ref, label_ref, whole_ref, half_ref):
+def prep_kernel(core_ref, prints_ref, marks_ref, whole_ref, half_ref):
     prints = prints_ref[...].T
     wide = prints.astype(F32)
     norm = jnp.sum(wide * wide, axis=0, keepdims=True)
@@ -79,32 +84,34 @@
     middle = rest.astype(BF16)
     low = (rest - middle.astype(F32)).astype(BF16)
     row = lax.broadcasted_iota(jnp.int32, (EXTRA, prints.shape[1]), 0)
-    extra = jnp.where(row == 0, potency_ref[...].astype(F32), 0.0)
-    extra = jnp.where(row == 1, label_ref[...].astype(F32), extra)
+    extra = jnp.where(row == 0, marks_ref[0:1, :], 0.0)
+    extra = jnp.where(row == 1, marks_ref[1:2, :], extra)
     for at, part in ((2, high), (3, middle), (4, low)):
         extra = jnp.where(row == at, part.astype(F32), extra)
     extra = extra.astype(BF16)
-    whole_ref[:BITS, :] = prints
-    whole_ref[BITS:, :] = extra
-    first = core_ref[0] == 0
     half = prints.shape[1] // 2
 
-    @pl.when(first)
+    def store(mine, other):
+        for ref in (whole_ref, half_ref):
+            ref[:BITS, :half] = prints[:, mine]
+            ref[BITS:, :half] = extra[:, mine]
+        whole_ref[:BITS, half:] = prints[:, other]
+        whole_ref[BITS:, half:] = extra[:, other]
+
+    @pl.when(core_ref[0] == 0)
     def _():
-        half_ref[:BITS, :] = prints[:, :half]
-        half_ref[BITS:, :] = extra[:, :half]
-
-    @pl.when(jnp.logical_not(first))
+        store(slice(0, half), slice(half, None))
+
+    @pl.when(core_ref[0] != 0)
     def _():
-        half_ref[:BITS, :] = prints[:, half:]
-        half_ref[BITS:, :] = extra[:, half:]
-
-
-def prepare(core, prints, potency, label):
+        store(slice(half, None), slice(0, half))
+
+
+def prepare(core, prints, marks):
     refs = prints.shape[0]
     return pl.pallas_call(
         prep_kernel,
-        in_specs=[pl.BlockSpec(memory_space=pltpu.SMEM), VMEM, VMEM, VMEM],
+        in_specs=[pl.BlockSpec(memory_space=pltpu.SMEM), VMEM, VMEM],
         out_specs=[VMEM, VMEM],
         out_shape=[
             jax.ShapeDtypeStruct((DEPTH, refs), BF16),
@@ -112,7 +119,7 @@
         ],
         compiler_params=params(),
         name="prepare",
-    )(core, prints, potency, label)
+    )(core, prints, marks)
 
 
 def piece_scores(queries, query_norm, piece_ref):
@@ -149,86 +156,80 @@
     return jnp.sum(wide * wide, axis=1, keepdims=True)
 
 
-def first_kernel(queries_ref, piece_ref, num_ref, den_ref, top_ref):
-    queries = queries_ref[...]
-    rows = queries.shape[0]
-    scores = piece_scores(queries, squared_norm(queries), piece_ref)
-    top = jnp.max(scores, axis=1, keepdims=True) + MARGIN
-    num = jnp.zeros((rows, TARGETS), F32)
-    den = jnp.zeros((rows, 128), F32)
-    num, den = add_piece(scores, top, piece_ref, num, den)
-    num_ref[...] = num
-    den_ref[...] = den
-    top_ref[...] = jnp.broadcast_to(top, (rows, 128))
-
-
-def more_kernel(count, *refs):
-    queries_ref, num_in, den_in, top_ref = refs[:4]
-    pieces = refs[4 : 4 + count]
-    num_ref, den_ref = refs[4 + count :]
+def unpack(state):
+    num, marks = state[:, :TARGETS], state[:, TARGETS:]
+    lane = lax.broadcasted_iota(jnp.int32, marks.shape, 1)
+    return num, jnp.where(lane == 1, marks, 0.0), marks[:, 0:1]
+
+
+def pack(num, den, top):
+    lane = lax.broadcasted_iota(jnp.int32, den.shape, 1)
+    marks = jnp.where(lane == 0, top, jnp.sum(den, axis=1, keepdims=True))
+    return jnp.concatenate([num, marks], axis=1)
+
+
+def empty(rows):
+    return jnp.zeros((rows, TARGETS), F32), jnp.zeros((rows, 128), F32)
+
+
+def add_pieces(queries_ref, state_in, state_ref, pieces):
     queries = queries_ref[...]
     query_norm = squared_norm(queries)
-    top = top_ref[:, 0:1]
-    num, den = num_in[...], den_in[...]
+    if state_in is None:
+        num, den = empty(queries.shape[0])
+        top = None
+    else:
+        num, den, top = unpack(state_in[...])
     for piece_ref in pieces:
         scores = piece_scores(queries, query_norm, piece_ref)
+        if top is None:
+            top = jnp.max(scores, axis=1, keepdims=True) + MARGIN
         num, den = add_piece(scores, top, piece_ref, num, den)
-    num_ref[...] = num
-    den_ref[...] = den
-
-
-def last_kernel(count, past, *refs):
-    queries_ref, num_in, den_in, top_ref, weight_ref = refs[:5]
-    pieces = refs[5 : 5 + count]
-    earlier = refs[5 + count : 5 + count + past]
-    profile_ref, moments_ref = refs[5 + count + past : 7 + count + past]
-    buffer, done = refs[7 + count + past :]
-    rows = queries_ref.shape[0]
-    queries = queries_ref[...]
-    query_norm = squared_norm(queries)
-    top = top_ref[:, 0:1]
-    num, den = num_in[...], den_in[...]
-    for piece_ref in pieces:
-        scores = piece_scores(queries, query_norm, piece_ref)
-        num, den = add_piece(scores, top, piece_ref, num, den)
-    total = jnp.sum(den, axis=1, keepdims=True)
-    profile_ref[...] = num * (1.0 / total)
-
-    @pl.when(jnp.logical_not(jnp.max(total) <= 1.0))
+    fits = jnp.max(den) <= 1.0
+
+    @pl.when(fits)
     def _():
-        width = pieces[0].shape[1]
-        sources = list(pieces)
-        for source in earlier:
-            sources += [source.at[:, pl.ds(k, width)] for k in range(0, source.shape[1], width)]
-        copies = [
-            pltpu.make_async_copy(source, buffer.at[k], done.at[k])
-            for k, source in enumerate(sources)
-        ]
-        for copy in copies:
-            copy.start()
-        for copy in copies:
-            copy.wait()
-
-        @pl.loop(0, rows // REDO)
+        state_ref[...] = pack(num, den, top)
+
+    @pl.when(jnp.logical_not(fits))
+    def _():
+        @pl.loop(0, queries_ref.shape[0] // REDO)
         def _(block):
             here = pl.ds(pl.multiple_of(block * REDO, REDO), REDO)
             queries = queries_ref[here, :]
             query_norm = squared_norm(queries)
-
-            def highest(k, best):
-                scores = piece_scores(queries, query_norm, buffer.at[k])
-                return jnp.maximum(best, jnp.max(scores, axis=1, keepdims=True))
-
-            def collect(k, sums):
-                scores = piece_scores(queries, query_norm, buffer.at[k])
-                return add_piece(scores, best, buffer.at[k], *sums)
-
-            best = lax.fori_loop(0, len(sources), highest, jnp.full((REDO, 1), -1.0, F32))
-            blank = jnp.zeros((REDO, TARGETS), F32), jnp.zeros((REDO, 128), F32)
-            num, den = lax.fori_loop(0, len(sources), collect, blank)
-            profile_ref[here, :] = num * (1.0 / jnp.sum(den, axis=1, keepdims=True))
-
-    profile = profile_ref[...]
+            best = jnp.zeros((REDO, 1), F32)
+            for piece_ref in pieces:
+                scores = piece_scores(queries, query_norm, piece_ref)
+                best = jnp.maximum(best, jnp.max(scores, axis=1, keepdims=True))
+            if state_in is None:
+                top = best + MARGIN
+                num, den = empty(REDO)
+            else:
+                num, den, old = unpack(state_in[here, :])
+                top = jnp.maximum(old, best + MARGIN)
+                scale = jnp.exp2(old - top)
+                num, den = num * scale, den * scale
+            for piece_ref in pieces:
+                scores = piece_scores(queries, query_norm, piece_ref)
+                num, den = add_piece(scores, top, piece_ref, num, den)
+            state_ref[here, :] = pack(num, den, top)
+
+
+def first_kernel(queries_ref, *refs):
+    add_pieces(queries_ref, None, refs[-1], refs[:-1])
+
+
+def more_kernel(queries_ref, state_in, *refs):
+    add_pieces(queries_ref, state_in, refs[-1], refs[:-1])
+
+
+def last_kernel(count, queries_ref, state_in, weight_ref, *refs):
+    state_ref, profile_ref, moments_ref = refs[count:]
+    add_pieces(queries_ref, state_in, state_ref, refs[:count])
+    num, den, _ = unpack(state_ref[...])
+    profile = num * (1.0 / jnp.sum(den, axis=1, keepdims=True))
+    profile_ref[...] = profile
     weight = weight_ref[...]
     weight_total = jnp.sum(weight, axis=0, keepdims=True)
     first = jnp.sum(profile * weight, axis=0, keepdims=True)
@@ -251,56 +252,54 @@
     return cost(6 * rows * refs * (BITS + TARGETS), rows * 2048 + refs * DEPTH * 2)
 
 
-def first_part(queries, piece):
+def state_shape(rows):
+    return jax.ShapeDtypeStruct((rows, TARGETS + 128), F32)
+
+
+def first_part(queries, pieces):
     rows = queries.shape[0]
     return pl.pallas_call(
         first_kernel,
-        in_specs=[VMEM, VMEM],
-        out_specs=[VMEM] * 3,
-        out_shape=[
-            jax.ShapeDtypeStruct((rows, TARGETS), F32),
-            jax.ShapeDtypeStruct((rows, 128), F32),
-            jax.ShapeDtypeStruct((rows, 128), F32),
-        ],
+        in_specs=[VMEM] * (1 + len(pieces)),
+        out_specs=VMEM,
+        out_shape=state_shape(rows),
         compiler_params=params(),
-        cost_estimate=work(rows, [piece]),
+        cost_estimate=work(rows, pieces),
         name="first_part",
-    )(queries, piece)
+    )(queries, *pieces)
 
 
 def more_part(queries, state, pieces):
     rows = queries.shape[0]
-    num, den = pl.pallas_call(
-        functools.partial(more_kernel, len(pieces)),
-        in_specs=[VMEM] * (4 + len(pieces)),
-        out_specs=[VMEM] * 2,
-        out_shape=[
-            jax.ShapeDtypeStruct((rows, TARGETS), F32),
-            jax.ShapeDtypeStruct((rows, 128), F32),
-        ],
+    return pl.pallas_call(
+        more_kernel,
+        in_specs=[VMEM] * (2 + len(pieces)),
+        out_specs=VMEM,
+        out_shape=state_shape(rows),
+        input_output_aliases={1: 0},
         compiler_params=params(),
         cost_estimate=work(rows, pieces),
         name="more_part",
-    )(queries, *state, *pieces)
-    return num, den, state[2]
-
-
-def last_part(queries, state, weight, pieces, earlier):
-    rows, width = queries.shape[0], pieces[0].shape[1]
-    count = sum(piece.shape[1] // width for piece in [*pieces, *earlier])
-    return pl.pallas_call(
-        functools.partial(last_kernel, len(pieces), len(earlier)),
-        in_specs=[VMEM] * (5 + len(pieces)) + [pl.BlockSpec(memory_space=pl.ANY)] * len(earlier),
-        out_specs=[VMEM] * 2,
+    )(queries, state, *pieces)
+
+
+def last_part(queries, state, weight, pieces):
+    rows = queries.shape[0]
+    _, profile, moments = pl.pallas_call(
+        functools.partial(last_kernel, len(pieces)),
+        in_specs=[VMEM] * (3 + len(pieces)),
+        out_specs=[VMEM] * 3,
         out_shape=[
+            state_shape(rows),
             jax.ShapeDtypeStruct((rows, TARGETS), F32),
             jax.ShapeDtypeStruct((TARGETS, TARGETS), F32),
         ],
-        scratch_shapes=[pltpu.VMEM((count, DEPTH, width), BF16), pltpu.SemaphoreType.DMA((count,))],
+        input_output_aliases={1: 0},
         compiler_params=params(),
         cost_estimate=work(rows, pieces),
         name="last_part",
-    )(queries, *state, weight, *pieces, *earlier)
+    )(queries, state, weight, *pieces)
+    return profile, moments
 
 
 def repeat_row(block, at):
@@ -442,41 +441,48 @@
     )(moments, profile, weight)
 
 
+def all_sum(moments):
+    plane, line = lax.axis_size(PLANE), lax.axis_size("z")
+    rows = TARGETS // plane
+    parts = lax.all_to_all(moments.reshape(plane, rows, TARGETS), PLANE, 0, 0)
+    part = jnp.sum(parts, axis=0, keepdims=True)
+    parts = lax.all_to_all(jnp.broadcast_to(part, (line, rows, TARGETS)), "z", 0, 0)
+    part = jnp.sum(parts, axis=0, keepdims=True)
+    parts = lax.all_to_all(jnp.broadcast_to(part, (plane, rows, TARGETS)), PLANE, 0, 0)
+    return parts.reshape(TARGETS, TARGETS)
+
+
 def on_device(compounds, compound_weight, reference_prints, potency, target_label):
-    devices = lax.axis_size(ALL)
-    core = lax.rem(lax.axis_index("lib"), 2).astype(jnp.int32).reshape(1)
+    core = lax.axis_index("core").astype(jnp.int32).reshape(1)
     weight = compound_weight[:, None]
-    own, half = prepare(core, reference_prints, potency[None, :], target_label[None, :])
+    marks = jnp.stack([potency.astype(F32), target_label.astype(F32)])
+    own, half = prepare(core, reference_prints, marks)
+    width = half.shape[1]
 
     hold = lax.optimization_barrier
-    far, flipped = send(half, up2), send(half, flip)
-    above, below = send(half, up), send(half, down)
-    state = first_part(compounds, own)
-    flipped, above, below, state = hold((flipped, above, below, state))
-    flipped_above, flipped_below = send(flipped, up), send(flipped, down)
-    others = [send(piece, sibling) for piece in (flipped, above, below)]
-    state = more_part(compounds, state, [flipped, above, below])
-    far, others, state = hold((far, others, state))
-    flipped_far, other_far = send(far, flip), send(far, sibling)
-    state = more_part(compounds, state, others + [far])
-    flipped_above, flipped_below, other_far, state = hold(
-        (flipped_above, flipped_below, other_far, state)
+    beside, flipped = send(own, onward), send(half, flip)
+    beside, flipped = hold((beside, flipped))
+    ahead, behind = send(flipped, up), send(flipped, down)
+    passing = beside[:, :width]
+    far, flipped_far = send(passing, onward), send(passing, across)
+    near = [beside, flipped, send(beside, sibling), send(flipped, sibling)]
+    state = first_part(compounds, [own] + near)
+    far, flipped_far, ahead, behind, state = hold((far, flipped_far, ahead, behind, state))
+    last = [far, flipped_far, ahead, behind]
+    others = [send(piece, sibling) for piece in last]
+    state = more_part(compounds, state, last)
+    profile, moments = last_part(compounds, state, weight, others)
+    return whiten(all_sum(moments), profile, weight)
+
+
+def solution(mesh):
+    sizes = dict(core=2, x_lo=2, x_hi=2)
+    sizes["z"] = mesh.shape["lib"] // (sizes["core"] * sizes["x_lo"])
+    sizes["y"] = mesh.shape["ref"] // sizes["x_hi"]
+    fine = jax.sharding.Mesh(mesh.devices.reshape([sizes[name] for name in ALL]), ALL)
+    spread = ALL
+    across_refs = ("y", "x_hi")
+    placed = (P(spread, None), P(spread), P(across_refs, None), P(across_refs), P(across_refs))
+    return jax.shard_map(
+        on_device, mesh=fine, in_specs=placed, out_specs=P(spread, None), check_vma=False
     )
-    other_above, other_below = send(flipped_above, sibling), send(flipped_below, sibling)
-    state = more_part(compounds, state, [other_far, flipped_above, flipped_below])
-    other_flipped_far = send(flipped_far, sibling)
-    later = [other_above, other_below, flipped_far, other_flipped_far]
-    earlier = [own, flipped, above, below, *others, far, other_far, flipped_above, flipped_below]
-    profile, moments = last_part(compounds, state, weight, later, earlier)
-
-    shares = lax.all_to_all(moments.reshape(devices, 2, TARGETS // 2), ALL, 0, 0)
-    share = jnp.sum(shares, axis=0, keepdims=True)
-    total = lax.all_to_all(jnp.broadcast_to(share, shares.shape), ALL, 0, 0)
-    return whiten(total.reshape(TARGETS, TARGETS), profile, weight)
-
-
-def solution(mesh):
-    placed = (P(("lib", "ref"), None), P(("lib", "ref")), P("ref", None), P("ref"), P("ref"))
-    return jax.shard_map(
-        on_device, mesh=mesh, in_specs=placed, out_specs=P(("lib", "ref"), None), check_vma=False
-    )

time: 188 us -> 112 us (0.60)
  Pallas kernels: 109 us -> 44.4 us
  starting transfers between devices: 22.7 us -> 13.6 us
  blocking collectives: 48.5 us -> 43.4 us
  waiting for transfers between devices: 4.75 us -> 7.03 us
    pallas_call x5 -> x3, Pallas kernels: 97.2 us -> 33.4 us  [the longest x1 14.1 us: first_part(): pl.pallas_call(first_kernel, in_specs=[VMEM] * (1 + len(pieces)), out_spe...]
    ppermute x14 -> x12, starting transfers between devices: 22.7 us -> 13.6 us  [send(): return lax.ppermute(value, ALL, route(move))]
    all_to_all x2 -> x3, blocking collectives: 48.5 us -> 43.4 us  [the longest x1 15.2 us: all_sum(): lax.all_to_all(jnp.broadcast_to(part, (line, rows, TARGETS)), 'z', 0, 0)]
    ppermute x14 -> x12, waiting for transfers between devices: 4.75 us -> 7.03 us  [send(): return lax.ppermute(value, ALL, route(move))]
  transfers between devices with their start and end apart: 14 -> 12, of which waited for: 2 -> 1; matrix products, arithmetic and copies ran while one was open for 0% -> 1% of each run, Pallas kernels for 5% -> 20%
where the time goes in v1:
time: 112 us
  Pallas kernels  44.4 us (40%)
  blocking collectives  43.4 us (39%)
  starting transfers between devices  13.6 us (12%)
  waiting for transfers between devices  7.03 us (6%)
  local copies, waits for them, and re-layouts  1.98 us (2%)
  other arithmetic  1.42 us (1%)
    all_to_all x1, blocking collectives, all_sum(): lax.all_to_all(jnp.broadcast_to(part, (line, rows, TARGETS)), 'z', 0, 0)  15.2 us
    pallas_call x1, Pallas kernels, first_part(): pl.pallas_call(first_kernel, in_specs=[VMEM] * (1 + len(pieces)), out_spe...  14.1 us
    all_to_all x1, blocking collectives, all_sum(): parts = lax.all_to_all(moments.reshape(plane, rows, TARGETS), PLANE, 0, 0)  14.1 us
    all_to_all x1, blocking collectives, all_sum(): lax.all_to_all(jnp.broadcast_to(part, (plane, rows, TARGETS)), PLANE, 0, 0)  14.1 us
    ppermute x12, starting transfers between devices, send(): return lax.ppermute(value, ALL, route(move))  13.6 us
    pallas_call x1, Pallas kernels, whiten(): pl.pallas_call(whiten_kernel, in_specs=[VMEM, VMEM, VMEM], out_specs=VMEM...  10.8 us
    pallas_call x1, Pallas kernels, last_part(): pl.pallas_call(functools.partial(last_kernel, len(pieces)), in_specs=[VME...  10.5 us
    pallas_call x1, Pallas kernels, more_part(): pl.pallas_call(more_kernel, in_specs=[VMEM] * (2 + len(pieces)), out_spec...  8.77 us
  transfers between devices with their start and end apart: 12, of which 1 were waited for; matrix products, arithmetic and copies ran while one was open for 1% of the time, Pallas kernels for 20%

profile of v1, /device:TPU:1, one launch (start us, length us, event | category | flops | bytes accessed | tf_op | source)
XLA Modules:
  0.0 112.0 jit_solution(7375308376776515570)
XLA Ops:
  0.0 0.7 stack.16
  0.7 0.7 convert_element_type.4
  1.4 0.0 copy-start
  1.4 1.0 copy-done
  2.4 0.3 prepare.1
  2.7 3.6 %collective-permute-start = (bf16[528,512]{1,0:T(8,128)(2,1)S(1)}, bf16[528,512]{1,0:T(8,128)(2,1)S(1)}, u32[]{:S(2)}, u32[]{:S(2)}) collective-permute-start(bf16[528,512]{1,0:T(8,128)(2,1)S(1)} %get-tuple-element.16.refs_0_), channel_id=1, source_target_pairs={{0,2},{1,3},{2,4},{3,5},{4,6},{5,7},{6,0},{7,1},{8,14},{9,15},{10,... | collective-permute-start | bytes 1622024 | tf_op jit(solution)/shard_map/ppermute | solution.py:51
  6.3 2.5 %collective-permute-start.1 = (bf16[528,256]{1,0:T(8,128)(2,1)S(1)}, bf16[528,256]{1,0:T(8,128)(2,1)S(1)}, u32[]{:S(2)}, u32[]{:S(2)}) collective-permute-start(bf16[528,256]{1,0:T(8,128)(2,1)S(1)} %get-tuple-element.17), channel_id=1, source_target_pairs={{0,17},{1,16},{2,19},{3,18},{4,21},{5,20},{6,23},{7,22},{8,25},{9,... | collective-permute-start | bytes 811016 | tf_op jit(solution)/shard_map/ppermute | solution.py:51
  8.8 7.0 %collective-permute-done.1.refs_2_ = bf16[528,256]{1,0:T(8,128)(2,1)S(1)} collective-permute-done((bf16[528,256]{1,0:T(8,128)(2,1)S(1)}, bf16[528,256]{1,0:T(8,128)(2,1)S(1)}, u32[]{:S(2)}, u32[]{:S(2)}) %collective-permute-start.1) | collective-permute-done | bytes 270368 | tf_op jit(solution)/shard_map/ppermute | solution.py:51
  15.8 0.8 collective-permute-start.6
  16.6 0.0 collective-permute-start.7
  16.6 0.9 copy.10.weight_ref
  17.5 2.6 %collective-permute-start.3 = (bf16[528,256]{1,0:T(8,128)(2,1)S(1)}, bf16[528,256]{1,0:T(8,128)(2,1)S(1)}, u32[]{:S(2)}, u32[]{:S(2)}) collective-permute-start(bf16[528,256]{1,0:T(8,128)(2,1)S(1)} %slice.3), channel_id=1, source_target_pairs={{0,19},{1,18},{2,21},{3,20},{4,23},{5,22},{6,17},{7,16},{8,31},{9,... | collective-permute-start | bytes 811016 | tf_op jit(solution)/shard_map/ppermute | solution.py:51
  20.1 0.2 collective-permute-start.2
  20.3 0.2 collective-permute-start.5
  20.5 0.0 collective-permute-done.7.refs_4_
  20.5 1.3 %collective-permute-start.4 = (bf16[528,256]{1,0:T(8,128)(2,1)S(1)}, bf16[528,256]{1,0:T(8,128)(2,1)S(1)}, u32[]{:S(2)}, u32[]{:S(2)}) collective-permute-start(bf16[528,256]{1,0:T(8,128)(2,1)S(1)} %collective-permute-done.1.refs_2_), channel_id=1, source_target_pairs={{0,2},{1,3},{2,4},{3,5},{4,6},{5,7},{6,0},{7,1},{8,10},{9,11},{10,... | collective-permute-start | bytes 811016 | tf_op jit(solution)/shard_map/ppermute | solution.py:51
  21.8 0.0 collective-permute-done.6.refs_3_
  21.8 14.1 %first_part.1.state_in = f32[1024,384]{1,0:T(8,128)S(1)} custom-call(bf16[1024,512]{1,0:T(8,128)(2,1)S(1)} %copy-done.1, bf16[528,512]{1,0:T(8,128)(2,1)S(1)} %get-tuple-element.16.refs_0_, bf16[528,512]{1,0:T(8,128)(2,1)S(1)} %collective-permute-done.refs_1_, bf16[528,256]{1,0:T(8,128)(2,1)S(1)} %collective-permute-done.1.refs_2_, ...), custom_call_target="tpu_custom_call" | custom-call | flops 9663676416 | bytes 4259840 | tf_op jit(solution)/shard_map/first_part/pallas_call | solution.py:261
  35.9 0.0 collective-permute-done.3.refs_1_
  35.9 0.0 collective-permute-done.5.refs_3_
  35.9 0.0 collective-permute-done.4.refs_2_
  35.9 1.7 %collective-permute-start.8 = (bf16[528,256]{1,0:T(8,128)(2,1)S(1)}, bf16[528,256]{1,0:T(8,128)(2,1)S(1)}, u32[]{:S(2)}, u32[]{:S(2)}) collective-permute-start(bf16[528,256]{1,0:T(8,128)(2,1)S(1)} %collective-permute-done.2.refs_0_), channel_id=1, source_target_pairs={{0,8},{1,9},{2,10},{3,11},{4,12},{5,13},{6,14},{7,15},{8,0},{9,1},... | collective-permute-start | bytes 811016 | tf_op jit(solution)/shard_map/ppermute | solution.py:51
  37.6 0.3 collective-permute-start.9
  37.9 0.2 collective-permute-start.10
  38.1 0.3 collective-permute-start.11
  38.4 8.8 %more_part.1.state_in = f32[1024,384]{1,0:T(8,128)S(1)} custom-call(bf16[1024,512]{1,0:T(8,128)(2,1)S(1)} %copy-done.1, f32[1024,384]{1,0:T(8,128)S(1)} %first_part.1.state_in, bf16[528,256]{1,0:T(8,128)(2,1)S(1)} %collective-permute-done.2.refs_0_, bf16[528,256]{1,0:T(8,128)(2,1)S(1)} %collective-permute-done.3.refs_1_, ...), custom_call_target="tpu_custom_call", output_to_operand_aliasing={{}: (1, {})} | custom-call | flops 4831838208 | bytes 3178496 | tf_op jit(solution)/shard_map/more_part/pallas_call | solution.py:274
  47.2 0.0 collective-permute-done.9.refs_1_
  47.2 10.5 %last_part.1 = (f32[1024,384]{1,0:T(8,128)S(1)}, f32[1024,256]{1,0:T(8,128)S(1)}, f32[256,256]{1,0:T(8,128)S(1)}) custom-call(bf16[1024,512]{1,0:T(8,128)(2,1)S(1)} %copy-done.1, f32[1024,384]{1,0:T(8,128)S(1)} %more_part.1.state_in, f32[1024,1]{1,0:T(8,128)S(1)} %copy.10.weight_ref, ...), custom_call_target="tpu_custom_call", output_to_operand_aliasing={{0}: (1, {})} | custom-call | flops 4831838208 | bytes 3178496 | tf_op jit(solution)/shard_map/last_part/pallas_call | solution.py:288
  57.7 14.1 %all_to_all.15 = f32[32,8,256]{2,1,0:T(8,128)S(1)} all-to-all(f32[32,8,256]{2,1,0:T(8,128)S(1)} %bitcast.7), channel_id=1, replica_groups=mesh['z'=8,'x_lo'=2,'core'=2,'y'=4,'x_hi'=2] {'x_lo','core','y','x_hi'}, dimensions={0} | all-to-all | bytes 524288 | tf_op jit(solution)/shard_map/all_to_all | solution.py:447
  71.9 15.2 %all_to_all.16 = f32[8,8,256]{2,1,0:T(8,128)S(1)} all-to-all(f32[8,8,256]{2,1,0:T(8,128)S(1)} %broadcast_in_dim.7), channel_id=1, replica_groups=mesh['z'=8,'x_lo'=2,'core'=2,'y'=4,'x_hi'=2] {'z'}, dimensions={0} | all-to-all | bytes 131072 | tf_op jit(solution)/shard_map/all_to_all | solution.py:449
  87.1 14.1 %all_to_all.17 = f32[32,8,256]{2,1,0:T(8,128)S(1)} all-to-all(f32[32,8,256]{2,1,0:T(8,128)S(1)} %broadcast_in_dim.8), channel_id=1, replica_groups=mesh['z'=8,'x_lo'=2,'core'=2,'y'=4,'x_hi'=2] {'x_lo','core','y','x_hi'}, dimensions={0} | all-to-all | bytes 524288 | tf_op jit(solution)/shard_map/all_to_all | solution.py:451
  101.2 10.8 %whiten.1 = f32[1024,256]{1,0:T(8,128)} custom-call(f32[256,256]{1,0:T(8,128)S(1)} %bitcast.6, f32[1024,256]{1,0:T(8,128)S(1)} %get-tuple-element.26.profile_ref, f32[1024,1]{1,0:T(8,128)S(1)} %copy.10.weight_ref), custom_call_target="tpu_custom_call" | custom-call | tf_op jit(solution)/shard_map/whiten/pallas_call | solution.py:434
  (13 shorter events, 0.1 us)
Async XLA Ops:
  1.4 1.0 copy-start
  2.4 19.3 %copy-start.1 = (bf16[1024,512]{1,0:T(8,128)(2,1)S(1)}, bf16[1024,512]{1,0:T(8,128)(2,1)}, u32[]{:S(2)}) copy-start(bf16[1024,512]{1,0:T(8,128)(2,1)} %queries_ref.5) | copy-start | bytes 3145732
  2.7 13.1 %collective-permute-start = (bf16[528,512]{1,0:T(8,128)(2,1)S(1)}, bf16[528,512]{1,0:T(8,128)(2,1)S(1)}, u32[]{:S(2)}, u32[]{:S(2)}) collective-permute-start(bf16[528,512]{1,0:T(8,128)(2,1)S(1)} %get-tuple-element.16.refs_0_), channel_id=1, source_target_pairs={{0,2},{1,3},{2,4},{3,5},{4,6},{5,7},{6,0},{7,1},{8,14},{9,15},{10,... | collective-permute-start | bytes 1622024 | tf_op jit(solution)/shard_map/ppermute | solution.py:51
  6.3 9.5 %collective-permute-start.1 = (bf16[528,256]{1,0:T(8,128)(2,1)S(1)}, bf16[528,256]{1,0:T(8,128)(2,1)S(1)}, u32[]{:S(2)}, u32[]{:S(2)}) collective-permute-start(bf16[528,256]{1,0:T(8,128)(2,1)S(1)} %get-tuple-element.17), channel_id=1, source_target_pairs={{0,17},{1,16},{2,19},{3,18},{4,21},{5,20},{6,23},{7,22},{8,25},{9,... | collective-permute-start | bytes 811016 | tf_op jit(solution)/shard_map/ppermute | solution.py:51
  15.8 6.0 %collective-permute-start.6 = (bf16[528,512]{1,0:T(8,128)(2,1)S(1)}, bf16[528,512]{1,0:T(8,128)(2,1)}, u32[]{:S(2)}, u32[]{:S(2)}) collective-permute-start(bf16[528,512]{1,0:T(8,128)(2,1)S(1)} %collective-permute-done.refs_1_), channel_id=1, source_target_pairs={{0,8},{1,9},{2,10},{3,11},{4,12},{5,13},{6,14},{7,15},{8,0},{9,1},... | collective-permute-start | bytes 1622024 | tf_op jit(solution)/shard_map/ppermute | solution.py:51
  16.6 3.9 %collective-permute-start.7 = (bf16[528,256]{1,0:T(8,128)(2,1)S(1)}, bf16[528,256]{1,0:T(8,128)(2,1)}, u32[]{:S(2)}, u32[]{:S(2)}) collective-permute-start(bf16[528,256]{1,0:T(8,128)(2,1)S(1)} %collective-permute-done.1.refs_2_), channel_id=1, source_target_pairs={{0,8},{1,9},{2,10},{3,11},{4,12},{5,13},{6,14},{7,15},{8,0},{9,1},... | collective-permute-start | bytes 811016 | tf_op jit(solution)/shard_map/ppermute | solution.py:51
  17.5 18.4 %collective-permute-start.3 = (bf16[528,256]{1,0:T(8,128)(2,1)S(1)}, bf16[528,256]{1,0:T(8,128)(2,1)S(1)}, u32[]{:S(2)}, u32[]{:S(2)}) collective-permute-start(bf16[528,256]{1,0:T(8,128)(2,1)S(1)} %slice.3), channel_id=1, source_target_pairs={{0,19},{1,18},{2,21},{3,20},{4,23},{5,22},{6,17},{7,16},{8,31},{9,... | collective-permute-start | bytes 811016 | tf_op jit(solution)/shard_map/ppermute | solution.py:51
  20.1 15.8 %collective-permute-start.2 = (bf16[528,256]{1,0:T(8,128)(2,1)S(1)}, bf16[528,256]{1,0:T(8,128)(2,1)S(1)}, u32[]{:S(2)}, u32[]{:S(2)}) collective-permute-start(bf16[528,256]{1,0:T(8,128)(2,1)S(1)} %slice.3), channel_id=1, source_target_pairs={{0,2},{1,3},{2,4},{3,5},{4,6},{5,7},{6,0},{7,1},{8,14},{9,15},{10,... | collective-permute-start | bytes 811016 | tf_op jit(solution)/shard_map/ppermute | solution.py:51
  20.3 15.6 %collective-permute-start.5 = (bf16[528,256]{1,0:T(8,128)(2,1)S(1)}, bf16[528,256]{1,0:T(8,128)(2,1)S(1)}, u32[]{:S(2)}, u32[]{:S(2)}) collective-permute-start(bf16[528,256]{1,0:T(8,128)(2,1)S(1)} %collective-permute-done.1.refs_2_), channel_id=1, source_target_pairs={{0,6},{1,7},{2,0},{3,1},{4,2},{5,3},{6,4},{7,5},{8,14},{9,15},{10,... | collective-permute-start | bytes 811016 | tf_op jit(solution)/shard_map/ppermute | solution.py:51
  20.5 15.5 %collective-permute-start.4 = (bf16[528,256]{1,0:T(8,128)(2,1)S(1)}, bf16[528,256]{1,0:T(8,128)(2,1)S(1)}, u32[]{:S(2)}, u32[]{:S(2)}) collective-permute-start(bf16[528,256]{1,0:T(8,128)(2,1)S(1)} %collective-permute-done.1.refs_2_), channel_id=1, source_target_pairs={{0,2},{1,3},{2,4},{3,5},{4,6},{5,7},{6,0},{7,1},{8,10},{9,11},{10,... | collective-permute-start | bytes 811016 | tf_op jit(solution)/shard_map/ppermute | solution.py:51
  35.9 11.3 %collective-permute-start.8 = (bf16[528,256]{1,0:T(8,128)(2,1)S(1)}, bf16[528,256]{1,0:T(8,128)(2,1)S(1)}, u32[]{:S(2)}, u32[]{:S(2)}) collective-permute-start(bf16[528,256]{1,0:T(8,128)(2,1)S(1)} %collective-permute-done.2.refs_0_), channel_id=1, source_target_pairs={{0,8},{1,9},{2,10},{3,11},{4,12},{5,13},{6,14},{7,15},{8,0},{9,1},... | collective-permute-start | bytes 811016 | tf_op jit(solution)/shard_map/ppermute | solution.py:51
  37.6 9.6 %collective-permute-start.9 = (bf16[528,256]{1,0:T(8,128)(2,1)S(1)}, bf16[528,256]{1,0:T(8,128)(2,1)S(1)}, u32[]{:S(2)}, u32[]{:S(2)}) collective-permute-start(bf16[528,256]{1,0:T(8,128)(2,1)S(1)} %collective-permute-done.3.refs_1_), channel_id=1, source_target_pairs={{0,8},{1,9},{2,10},{3,11},{4,12},{5,13},{6,14},{7,15},{8,0},{9,1},... | collective-permute-start | bytes 811016 | tf_op jit(solution)/shard_map/ppermute | solution.py:51
  37.9 9.3 %collective-permute-start.10 = (bf16[528,256]{1,0:T(8,128)(2,1)S(1)}, bf16[528,256]{1,0:T(8,128)(2,1)S(1)}, u32[]{:S(2)}, u32[]{:S(2)}) collective-permute-start(bf16[528,256]{1,0:T(8,128)(2,1)S(1)} %collective-permute-done.4.refs_2_), channel_id=1, source_target_pairs={{0,8},{1,9},{2,10},{3,11},{4,12},{5,13},{6,14},{7,15},{8,0},{9,1},... | collective-permute-start | bytes 811016 | tf_op jit(solution)/shard_map/ppermute | solution.py:51
  38.1 9.1 %collective-permute-start.11 = (bf16[528,256]{1,0:T(8,128)(2,1)S(1)}, bf16[528,256]{1,0:T(8,128)(2,1)S(1)}, u32[]{:S(2)}, u32[]{:S(2)}) collective-permute-start(bf16[528,256]{1,0:T(8,128)(2,1)S(1)} %collective-permute-done.5.refs_3_), channel_id=1, source_target_pairs={{0,8},{1,9},{2,10},{3,11},{4,12},{5,13},{6,14},{7,15},{8,0},{9,1},... | collective-permute-start | bytes 811016 | tf_op jit(solution)/shard_map/ppermute | solution.py:51

commit v2 on v1

--- a/solution.py
+++ b/solution.py
@@ -51,14 +51,6 @@
     return lax.ppermute(value, ALL, route(move))
 
 
-def up(x, y, z, c):
-    return x, y + 1, z, c
-
-
-def down(x, y, z, c):
-    return x, y - 1, z, c
-
-
 def flip(x, y, z, c):
     return 3 - x, y, z, c
 
@@ -75,7 +67,7 @@
     return x, y, z, 1 - c
 
 
-def prep_kernel(core_ref, prints_ref, marks_ref, whole_ref, half_ref):
+def prep_kernel(core_ref, prints_ref, marks_ref, mine_ref, other_ref):
     prints = prints_ref[...].T
     wide = prints.astype(F32)
     norm = jnp.sum(wide * wide, axis=0, keepdims=True)
@@ -83,20 +75,20 @@
     rest = norm - high.astype(F32)
     middle = rest.astype(BF16)
     low = (rest - middle.astype(F32)).astype(BF16)
+    marks = marks_ref[...]
+    label = jnp.floor(marks * (1.0 / 16.0))
     row = lax.broadcasted_iota(jnp.int32, (EXTRA, prints.shape[1]), 0)
-    extra = jnp.where(row == 0, marks_ref[0:1, :], 0.0)
-    extra = jnp.where(row == 1, marks_ref[1:2, :], extra)
+    extra = jnp.where(row == 0, marks - 16.0 * label, 0.0)
+    extra = jnp.where(row == 1, label, extra)
     for at, part in ((2, high), (3, middle), (4, low)):
         extra = jnp.where(row == at, part.astype(F32), extra)
     extra = extra.astype(BF16)
     half = prints.shape[1] // 2
 
     def store(mine, other):
-        for ref in (whole_ref, half_ref):
-            ref[:BITS, :half] = prints[:, mine]
-            ref[BITS:, :half] = extra[:, mine]
-        whole_ref[:BITS, half:] = prints[:, other]
-        whole_ref[BITS:, half:] = extra[:, other]
+        for ref, part in ((mine_ref, mine), (other_ref, other)):
+            ref[:BITS, :] = prints[:, part]
+            ref[BITS:, :] = extra[:, part]
 
     @pl.when(core_ref[0] == 0)
     def _():
@@ -108,15 +100,12 @@
 
 
 def prepare(core, prints, marks):
-    refs = prints.shape[0]
+    shape = jax.ShapeDtypeStruct((DEPTH, prints.shape[0] // 2), BF16)
     return pl.pallas_call(
         prep_kernel,
         in_specs=[pl.BlockSpec(memory_space=pltpu.SMEM), VMEM, VMEM],
         out_specs=[VMEM, VMEM],
-        out_shape=[
-            jax.ShapeDtypeStruct((DEPTH, refs), BF16),
-            jax.ShapeDtypeStruct((DEPTH, refs // 2), BF16),
-        ],
+        out_shape=[shape, shape],
         compiler_params=params(),
         name="prepare",
     )(core, prints, marks)
@@ -159,12 +148,13 @@
 def unpack(state):
     num, marks = state[:, :TARGETS], state[:, TARGETS:]
     lane = lax.broadcasted_iota(jnp.int32, marks.shape, 1)
-    return num, jnp.where(lane == 1, marks, 0.0), marks[:, 0:1]
-
-
-def pack(num, den, top):
+    return num, jnp.where(lane == 1, marks, 0.0), marks[:, 0:1], marks[:, 2:3]
+
+
+def pack(num, den, top, weight):
     lane = lax.broadcasted_iota(jnp.int32, den.shape, 1)
     marks = jnp.where(lane == 0, top, jnp.sum(den, axis=1, keepdims=True))
+    marks = jnp.where(lane == 2, weight, marks)
     return jnp.concatenate([num, marks], axis=1)
 
 
@@ -172,14 +162,14 @@
     return jnp.zeros((rows, TARGETS), F32), jnp.zeros((rows, 128), F32)
 
 
-def add_pieces(queries_ref, state_in, state_ref, pieces):
+def add_pieces(queries_ref, state_in, state_ref, pieces, weight=None):
     queries = queries_ref[...]
     query_norm = squared_norm(queries)
     if state_in is None:
         num, den = empty(queries.shape[0])
         top = None
     else:
-        num, den, top = unpack(state_in[...])
+        num, den, top, weight = unpack(state_in[...])
     for piece_ref in pieces:
         scores = piece_scores(queries, query_norm, piece_ref)
         if top is None:
@@ -189,10 +179,13 @@
 
     @pl.when(fits)
     def _():
-        state_ref[...] = pack(num, den, top)
+        state_ref[...] = pack(num, den, top, weight)
 
     @pl.when(jnp.logical_not(fits))
     def _():
+        if state_in is None:
+            state_ref[...] = pack(num, den, top, weight)
+
         @pl.loop(0, queries_ref.shape[0] // REDO)
         def _(block):
             here = pl.ds(pl.multiple_of(block * REDO, REDO), REDO)
@@ -205,40 +198,50 @@
             if state_in is None:
                 top = best + MARGIN
                 num, den = empty(REDO)
+                weight = unpack(state_ref[here, :])[3]
             else:
-                num, den, old = unpack(state_in[here, :])
+                num, den, old, weight = unpack(state_in[here, :])
                 top = jnp.maximum(old, best + MARGIN)
                 scale = jnp.exp2(old - top)
                 num, den = num * scale, den * scale
             for piece_ref in pieces:
                 scores = piece_scores(queries, query_norm, piece_ref)
                 num, den = add_piece(scores, top, piece_ref, num, den)
-            state_ref[here, :] = pack(num, den, top)
-
-
-def first_kernel(queries_ref, *refs):
-    add_pieces(queries_ref, None, refs[-1], refs[:-1])
+            state_ref[here, :] = pack(num, den, top, weight)
+
+
+def first_kernel(queries_ref, weight_ref, *refs):
+    columns = weight_ref[...].T
+    weight = jnp.concatenate([columns[:, k : k + 1] for k in range(columns.shape[1])], axis=0)
+    add_pieces(queries_ref, None, refs[-1], refs[:-1], weight)
 
 
 def more_kernel(queries_ref, state_in, *refs):
     add_pieces(queries_ref, state_in, refs[-1], refs[:-1])
 
 
-def last_kernel(count, queries_ref, state_in, weight_ref, *refs):
-    state_ref, profile_ref, moments_ref = refs[count:]
+def split(value):
+    high = value.astype(BF16)
+    return high, (value - high.astype(F32)).astype(BF16)
+
+
+def last_kernel(count, queries_ref, state_in, *refs):
+    state_ref, moments_ref = refs[count:]
     add_pieces(queries_ref, state_in, state_ref, refs[:count])
-    num, den, _ = unpack(state_ref[...])
+    num, den, _, weight = unpack(state_ref[...])
     profile = num * (1.0 / jnp.sum(den, axis=1, keepdims=True))
-    profile_ref[...] = profile
-    weight = weight_ref[...]
+    state_ref[:, :TARGETS] = profile
     weight_total = jnp.sum(weight, axis=0, keepdims=True)
     first = jnp.sum(profile * weight, axis=0, keepdims=True)
     mean = first / weight_total
     spread = (profile - mean) * jnp.sqrt(weight)
     outer = (((0,), (0,)), ((), ()))
-    moments = lax.dot_general(
-        spread, spread, outer, precision=EXACT, preferred_element_type=F32
-    ) + lax.dot_general(mean, first, outer, precision=EXACT, preferred_element_type=F32)
+    high, low = split(spread)
+    cross = lax.dot_general(high, low, outer, preferred_element_type=F32)
+    moments = lax.dot_general(high, high, outer, preferred_element_type=F32) + (cross + cross.T)
+    moments = moments + lax.dot_general(
+        mean, first, outer, precision=EXACT, preferred_element_type=F32
+    )
     row = lax.broadcasted_iota(jnp.int32, (TARGETS, TARGETS), 0)
     column = lax.broadcasted_iota(jnp.int32, (TARGETS, TARGETS), 1)
     moments = jnp.where((row == 0) & (column > 0), first, moments)
@@ -256,17 +259,17 @@
     return jax.ShapeDtypeStruct((rows, TARGETS + 128), F32)
 
 
-def first_part(queries, pieces):
+def first_part(queries, weight, pieces):
     rows = queries.shape[0]
     return pl.pallas_call(
         first_kernel,
-        in_specs=[VMEM] * (1 + len(pieces)),
+        in_specs=[VMEM] * (2 + len(pieces)),
         out_specs=VMEM,
         out_shape=state_shape(rows),
         compiler_params=params(),
         cost_estimate=work(rows, pieces),
         name="first_part",
-    )(queries, *pieces)
+    )(queries, weight.reshape(rows // 128, 128), *pieces)
 
 
 def more_part(queries, state, pieces):
@@ -283,23 +286,18 @@
     )(queries, state, *pieces)
 
 
-def last_part(queries, state, weight, pieces):
+def last_part(queries, state, pieces):
     rows = queries.shape[0]
-    _, profile, moments = pl.pallas_call(
+    return pl.pallas_call(
         functools.partial(last_kernel, len(pieces)),
-        in_specs=[VMEM] * (3 + len(pieces)),
-        out_specs=[VMEM] * 3,
-        out_shape=[
-            state_shape(rows),
-            jax.ShapeDtypeStruct((rows, TARGETS), F32),
-            jax.ShapeDtypeStruct((TARGETS, TARGETS), F32),
-        ],
+        in_specs=[VMEM] * (2 + len(pieces)),
+        out_specs=[VMEM] * 2,
+        out_shape=[state_shape(rows), jax.ShapeDtypeStruct((TARGETS, TARGETS), F32)],
         input_output_aliases={1: 0},
         compiler_params=params(),
         cost_estimate=work(rows, pieces),
         name="last_part",
-    )(queries, state, weight, *pieces)
-    return profile, moments
+    )(queries, state, *pieces)
 
 
 def repeat_row(block, at):
@@ -409,7 +407,7 @@
     return jnp.concatenate(result, axis=0)
 
 
-def whiten_kernel(moments_ref, profile_ref, weight_ref, out_ref):
+def whiten_kernel(moments_ref, state_ref, out_ref):
     total = moments_ref[...]
     row = lax.broadcasted_iota(jnp.int32, (TARGETS, TARGETS), 0)
     column = lax.broadcasted_iota(jnp.int32, (TARGETS, TARGETS), 1)
@@ -424,21 +422,26 @@
     covariance = (lower + strict.T) * share - outer
     covariance = covariance + jnp.where(row == column, SHRINKAGE, 0.0)
     inverse = inverse_factor(covariance, TARGETS)
-    centered = (profile_ref[...] - mean) * jnp.sqrt(weight_ref[...])
-    out_ref[...] = lax.dot_general(
-        centered, inverse, (((1,), (1,)), ((), ())), precision=EXACT, preferred_element_type=F32
-    )
-
-
-def whiten(moments, profile, weight):
+    profile, _, _, weight = unpack(state_ref[...])
+    centered = split((profile - mean) * jnp.sqrt(weight))
+    inverse = split(inverse)
+
+    def product(a, b):
+        return lax.dot_general(a, b, (((1,), (1,)), ((), ())), preferred_element_type=F32)
+
+    cross = product(centered[0], inverse[1]) + product(centered[1], inverse[0])
+    out_ref[...] = product(centered[0], inverse[0]) + cross
+
+
+def whiten(moments, state):
     return pl.pallas_call(
         whiten_kernel,
-        in_specs=[VMEM, VMEM, VMEM],
+        in_specs=[VMEM, VMEM],
         out_specs=VMEM,
-        out_shape=jax.ShapeDtypeStruct(profile.shape, F32),
+        out_shape=jax.ShapeDtypeStruct((state.shape[0], TARGETS), F32),
         compiler_params=params(),
         name="whiten",
-    )(moments, profile, weight)
+    )(moments, state)
 
 
 def all_sum(moments):
@@ -454,25 +457,22 @@
 
 def on_device(compounds, compound_weight, reference_prints, potency, target_label):
     core = lax.axis_index("core").astype(jnp.int32).reshape(1)
-    weight = compound_weight[:, None]
-    marks = jnp.stack([potency.astype(F32), target_label.astype(F32)])
-    own, half = prepare(core, reference_prints, marks)
-    width = half.shape[1]
+    marks = target_label.astype(F32) * 16.0 + potency.astype(F32)
+    mine, other = prepare(core, reference_prints, marks[None, :])
 
     hold = lax.optimization_barrier
-    beside, flipped = send(own, onward), send(half, flip)
-    beside, flipped = hold((beside, flipped))
-    ahead, behind = send(flipped, up), send(flipped, down)
-    passing = beside[:, :width]
-    far, flipped_far = send(passing, onward), send(passing, across)
-    near = [beside, flipped, send(beside, sibling), send(flipped, sibling)]
-    state = first_part(compounds, [own] + near)
-    far, flipped_far, ahead, behind, state = hold((far, flipped_far, ahead, behind, state))
-    last = [far, flipped_far, ahead, behind]
+    beside, flipped, rest = send(mine, onward), send(mine, flip), send(other, onward)
+    far, flipped_far = send(beside, onward), send(beside, across)
+    ahead, ahead_rest = send(flipped, onward), send(rest, flip)
+    near = [beside, flipped, rest]
+    near += [send(piece, sibling) for piece in near]
+    state = first_part(compounds, compound_weight, [mine, other] + near)
+    far, flipped_far, ahead, ahead_rest, state = hold((far, flipped_far, ahead, ahead_rest, state))
+    last = [far, flipped_far, ahead, ahead_rest]
     others = [send(piece, sibling) for piece in last]
     state = more_part(compounds, state, last)
-    profile, moments = last_part(compounds, state, weight, others)
-    return whiten(all_sum(moments), profile, weight)
+    state, moments = last_part(compounds, state, others)
+    return whiten(all_sum(moments), state)
 
 
 def solution(mesh):

time: 112 us -> 112 us (level)
  waiting for transfers between devices: 7.03 us -> 2.62 us
  starting transfers between devices: 13.6 us -> 17.2 us
  blocking collectives: 43.4 us -> 44.7 us
    ppermute x12 -> x14, waiting for transfers between devices: 7.03 us -> 2.62 us  [send(): return lax.ppermute(value, ALL, route(move))]
    ppermute x12 -> x14, starting transfers between devices: 13.6 us -> 17.2 us  [send(): return lax.ppermute(value, ALL, route(move))]
    unnamed x4 -> x8, local copies, waits for them, and re-layouts: 1.04 us -> 2.96 us
    all_to_all x1, blocking collectives: 14.1 us -> 15.4 us  [all_sum(): parts = lax.all_to_all(moments.reshape(plane, rows, TARGETS), PLANE, 0, 0)]
  transfers between devices with their start and end apart: 12 -> 14, of which waited for: 1 -> 2; matrix products, arithmetic and copies ran while one was open for 1% -> 0% of each run, Pallas kernels for 20% -> 20%
where the time goes in v2:
time: 112 us
  blocking collectives  44.7 us (40%)
  Pallas kernels  43.5 us (39%)
  starting transfers between devices  17.2 us (15%)
  local copies, waits for them, and re-layouts  2.98 us (3%)
  waiting for transfers between devices  2.62 us (2%)
    ppermute x14, starting transfers between devices, send(): return lax.ppermute(value, ALL, route(move))  17.2 us
    all_to_all x1, blocking collectives, all_sum(): parts = lax.all_to_all(moments.reshape(plane, rows, TARGETS), PLANE, 0, 0)  15.4 us
    all_to_all x1, blocking collectives, all_sum(): lax.all_to_all(jnp.broadcast_to(part, (line, rows, TARGETS)), 'z', 0, 0)  15.3 us
    pallas_call x1, Pallas kernels, first_part(): pl.pallas_call(first_kernel, in_specs=[VMEM] * (2 + len(pieces)), out_spe...  14.2 us
    all_to_all x1, blocking collectives, all_sum(): lax.all_to_all(jnp.broadcast_to(part, (plane, rows, TARGETS)), PLANE, 0, 0)  14.1 us
    pallas_call x1, Pallas kernels, whiten(): pl.pallas_call(whiten_kernel, in_specs=[VMEM, VMEM], out_specs=VMEM, out_...  10.5 us
    pallas_call x1, Pallas kernels, last_part(): pl.pallas_call(functools.partial(last_kernel, len(pieces)), in_specs=[VME...  9.96 us
    pallas_call x1, Pallas kernels, more_part(): pl.pallas_call(more_kernel, in_specs=[VMEM] * (2 + len(pieces)), out_spec...  8.65 us
  transfers between devices with their start and end apart: 14, of which 2 were waited for; matrix products, arithmetic and copies ran while one was open for 0% of the time, Pallas kernels for 20%

profile of v2, /device:TPU:1, one launch (start us, length us, event | category | flops | bytes accessed | tf_op | source)
XLA Modules:
  0.0 111.9 jit_solution(7774559114325269863)
XLA Ops:
  0.0 0.7 convert_add_fusion
  0.7 1.0 copy-done
  1.7 0.2 prepare.1
  2.0 3.6 %collective-permute-start.5 = (bf16[528,256]{1,0:T(8,128)(2,1)S(1)}, bf16[528,256]{1,0:T(8,128)(2,1)S(1)}, u32[]{:S(2)}, u32[]{:S(2)}) collective-permute-start(bf16[528,256]{1,0:T(8,128)(2,1)S(1)} %get-tuple-element.15.refs_1_), channel_id=1, source_target_pairs={{0,2},{1,3},{2,4},{3,5},{4,6},{5,7},{6,0},{7,1},{8,14},{9,15},{10,... | collective-permute-start | bytes 811016 | tf_op jit(solution)/shard_map/ppermute | solution.py:51
  5.6 2.5 %collective-permute-start.3 = (bf16[528,256]{1,0:T(8,128)(2,1)S(1)}, bf16[528,256]{1,0:T(8,128)(2,1)S(1)}, u32[]{:S(2)}, u32[]{:S(2)}) collective-permute-start(bf16[528,256]{1,0:T(8,128)(2,1)S(1)} %get-tuple-element.14.refs_0_), channel_id=1, source_target_pairs={{0,17},{1,16},{2,19},{3,18},{4,21},{5,20},{6,23},{7,22},{8,25},{9,... | collective-permute-start | bytes 811016 | tf_op jit(solution)/shard_map/ppermute | solution.py:51
  8.1 0.5 collective-permute-start
  8.6 0.5 collective-permute-done.5.refs_4_
  9.0 3.9 %collective-permute-start.9 = (bf16[528,256]{1,0:T(8,128)(2,1)S(1)}, bf16[528,256]{1,0:T(8,128)(2,1)S(1)}, u32[]{:S(2)}, u32[]{:S(2)}) collective-permute-start(bf16[528,256]{1,0:T(8,128)(2,1)S(1)} %collective-permute-done.5.refs_4_), channel_id=1, source_target_pairs={{0,8},{1,9},{2,10},{3,11},{4,12},{5,13},{6,14},{7,15},{8,0},{9,1},... | collective-permute-start | bytes 811016 | tf_op jit(solution)/shard_map/ppermute | solution.py:51
  13.0 2.1 %collective-permute-done.3.refs_3_ = bf16[528,256]{1,0:T(8,128)(2,1)S(1)} collective-permute-done((bf16[528,256]{1,0:T(8,128)(2,1)S(1)}, bf16[528,256]{1,0:T(8,128)(2,1)S(1)}, u32[]{:S(2)}, u32[]{:S(2)}) %collective-permute-start.3) | collective-permute-done | bytes 270368 | tf_op jit(solution)/shard_map/ppermute | solution.py:51
  15.1 0.6 collective-permute-start.8
  15.7 0.1 collective-permute-start.7
  15.9 2.4 %collective-permute-start.6 = (bf16[528,256]{1,0:T(8,128)(2,1)S(1)}, bf16[528,256]{1,0:T(8,128)(2,1)S(1)}, u32[]{:S(2)}, u32[]{:S(2)}) collective-permute-start(bf16[528,256]{1,0:T(8,128)(2,1)S(1)} %collective-permute-done.5.refs_4_), channel_id=1, source_target_pairs={{0,17},{1,16},{2,19},{3,18},{4,21},{5,20},{6,23},{7,22},{8,25},{9,... | collective-permute-start | bytes 811016 | tf_op jit(solution)/shard_map/ppermute | solution.py:51
  18.3 0.4 collective-permute-start.4
  18.7 1.0 collective-permute-start.2
  19.7 0.0 collective-permute-done.8.refs_6_
  19.7 0.5 collective-permute-start.1
  20.1 1.2 %copy-done.1 = bf16[1024,512]{1,0:T(8,128)(2,1)S(1)} copy-done((bf16[1024,512]{1,0:T(8,128)(2,1)S(1)}, bf16[1024,512]{1,0:T(8,128)(2,1)}, u32[]{:S(2)}) %copy-start.1) | copy-done | bytes 1048600
  21.4 0.7 copy-done.3
  22.1 14.2 %first_part.1.state_in = f32[1024,384]{1,0:T(8,128)S(1)} custom-call(bf16[1024,512]{1,0:T(8,128)(2,1)S(1)} %copy-done.1, f32[8,128]{1,0:T(8,128)S(1)} %bitcast.8, bf16[528,256]{1,0:T(8,128)(2,1)S(1)} %get-tuple-element.14.refs_0_, bf16[528,256]{1,0:T(8,128)(2,1)S(1)} %get-tuple-element.15.refs_1_, bf16[528,256]{1,0:T(8,128)(2,1)S(1)} %collective-permute-done.refs_2_, ...), custom_call_target="tpu_custom_call" | custom-call | flops 9663676416 | bytes 4259840 | tf_op jit(solution)/shard_map/first_part/pallas_call | solution.py:264
  36.2 0.0 copy-start.2
  36.3 0.0 collective-permute-done.6.refs_3_
  36.3 0.0 collective-permute-done.2.refs_1_
  36.3 1.1 collective-permute-start.10
  37.4 0.1 collective-permute-start.11
  37.5 0.4 collective-permute-start.12
  37.9 0.1 collective-permute-start.13
  38.0 8.7 %more_part.1.state_in = f32[1024,384]{1,0:T(8,128)S(1)} custom-call(bf16[1024,512]{1,0:T(8,128)(2,1)S(1)} %copy-done.1, f32[1024,384]{1,0:T(8,128)S(1)} %first_part.1.state_in, bf16[528,256]{1,0:T(8,128)(2,1)S(1)} %collective-permute-done.1.refs_0_, bf16[528,256]{1,0:T(8,128)(2,1)S(1)} %collective-permute-done.2.refs_1_, ...), custom_call_target="tpu_custom_call", output_to_operand_aliasing={{}: (1, {})} | custom-call | flops 4831838208 | bytes 3178496 | tf_op jit(solution)/shard_map/more_part/pallas_call | solution.py:277
  46.7 10.0 %last_part.1 = (f32[1024,384]{1,0:T(8,128)S(1)}, f32[256,256]{1,0:T(8,128)S(1)}) custom-call(bf16[1024,512]{1,0:T(8,128)(2,1)S(1)} %copy-done.2, f32[1024,384]{1,0:T(8,128)S(1)} %more_part.1.state_in, bf16[528,256]{1,0:T(8,128)(2,1)S(1)} %collective-permute-done.10.refs_0_, ...), custom_call_target="tpu_custom_call", output_to_operand_aliasing={{0}: (1, {})} | custom-call | flops 4831838208 | bytes 3178496 | tf_op jit(solution)/shard_map/last_part/pallas_call | solution.py:291
  56.6 15.4 %all_to_all.15 = f32[32,8,256]{2,1,0:T(8,128)S(1)} all-to-all(f32[32,8,256]{2,1,0:T(8,128)S(1)} %bitcast.6), channel_id=1, replica_groups=mesh['z'=8,'x_lo'=2,'core'=2,'y'=4,'x_hi'=2] {'x_lo','core','y','x_hi'}, dimensions={0} | all-to-all | bytes 524288 | tf_op jit(solution)/shard_map/all_to_all | solution.py:450
  72.1 15.3 %all_to_all.16 = f32[8,8,256]{2,1,0:T(8,128)S(1)} all-to-all(f32[8,8,256]{2,1,0:T(8,128)S(1)} %broadcast_in_dim.7), channel_id=1, replica_groups=mesh['z'=8,'x_lo'=2,'core'=2,'y'=4,'x_hi'=2] {'z'}, dimensions={0} | all-to-all | bytes 131072 | tf_op jit(solution)/shard_map/all_to_all | solution.py:452
  87.4 14.1 %all_to_all.17 = f32[32,8,256]{2,1,0:T(8,128)S(1)} all-to-all(f32[32,8,256]{2,1,0:T(8,128)S(1)} %broadcast_in_dim.8), channel_id=1, replica_groups=mesh['z'=8,'x_lo'=2,'core'=2,'y'=4,'x_hi'=2] {'x_lo','core','y','x_hi'}, dimensions={0} | all-to-all | bytes 524288 | tf_op jit(solution)/shard_map/all_to_all | solution.py:454
  101.5 10.5 %whiten.1 = f32[1024,256]{1,0:T(8,128)} custom-call(f32[256,256]{1,0:T(8,128)S(1)} %bitcast.5, f32[1024,384]{1,0:T(8,128)S(1)} %get-tuple-element.22.state_ref), custom_call_target="tpu_custom_call" | custom-call | tf_op jit(solution)/shard_map/whiten/pallas_call | solution.py:437
  (17 shorter events, 0.1 us)
Async XLA Ops:
  0.7 1.0 copy-start
  2.0 7.0 %collective-permute-start.5 = (bf16[528,256]{1,0:T(8,128)(2,1)S(1)}, bf16[528,256]{1,0:T(8,128)(2,1)S(1)}, u32[]{:S(2)}, u32[]{:S(2)}) collective-permute-start(bf16[528,256]{1,0:T(8,128)(2,1)S(1)} %get-tuple-element.15.refs_1_), channel_id=1, source_target_pairs={{0,2},{1,3},{2,4},{3,5},{4,6},{5,7},{6,0},{7,1},{8,14},{9,15},{10,... | collective-permute-start | bytes 811016 | tf_op jit(solution)/shard_map/ppermute | solution.py:51
  5.6 9.5 %collective-permute-start.3 = (bf16[528,256]{1,0:T(8,128)(2,1)S(1)}, bf16[528,256]{1,0:T(8,128)(2,1)S(1)}, u32[]{:S(2)}, u32[]{:S(2)}) collective-permute-start(bf16[528,256]{1,0:T(8,128)(2,1)S(1)} %get-tuple-element.14.refs_0_), channel_id=1, source_target_pairs={{0,17},{1,16},{2,19},{3,18},{4,21},{5,20},{6,23},{7,22},{8,25},{9,... | collective-permute-start | bytes 811016 | tf_op jit(solution)/shard_map/ppermute | solution.py:51
  8.1 7.6 %collective-permute-start = (bf16[528,256]{1,0:T(8,128)(2,1)S(1)}, bf16[528,256]{1,0:T(8,128)(2,1)S(1)}, u32[]{:S(2)}, u32[]{:S(2)}) collective-permute-start(bf16[528,256]{1,0:T(8,128)(2,1)S(1)} %get-tuple-element.14.refs_0_), channel_id=1, source_target_pairs={{0,2},{1,3},{2,4},{3,5},{4,6},{5,7},{6,0},{7,1},{8,14},{9,15},{10,... | collective-permute-start | bytes 811016 | tf_op jit(solution)/shard_map/ppermute | solution.py:51
  9.0 9.7 %collective-permute-start.9 = (bf16[528,256]{1,0:T(8,128)(2,1)S(1)}, bf16[528,256]{1,0:T(8,128)(2,1)S(1)}, u32[]{:S(2)}, u32[]{:S(2)}) collective-permute-start(bf16[528,256]{1,0:T(8,128)(2,1)S(1)} %collective-permute-done.5.refs_4_), channel_id=1, source_target_pairs={{0,8},{1,9},{2,10},{3,11},{4,12},{5,13},{6,14},{7,15},{8,0},{9,1},... | collective-permute-start | bytes 811016 | tf_op jit(solution)/shard_map/ppermute | solution.py:51
  15.1 4.6 %collective-permute-start.8 = (bf16[528,256]{1,0:T(8,128)(2,1)S(1)}, bf16[528,256]{1,0:T(8,128)(2,1)S(1)}, u32[]{:S(2)}, u32[]{:S(2)}) collective-permute-start(bf16[528,256]{1,0:T(8,128)(2,1)S(1)} %collective-permute-done.3.refs_3_), channel_id=1, source_target_pairs={{0,8},{1,9},{2,10},{3,11},{4,12},{5,13},{6,14},{7,15},{8,0},{9,1},... | collective-permute-start | bytes 811016 | tf_op jit(solution)/shard_map/ppermute | solution.py:51
  15.7 4.4 %collective-permute-start.7 = (bf16[528,256]{1,0:T(8,128)(2,1)S(1)}, bf16[528,256]{1,0:T(8,128)(2,1)S(1)}, u32[]{:S(2)}, u32[]{:S(2)}) collective-permute-start(bf16[528,256]{1,0:T(8,128)(2,1)S(1)} %collective-permute-done.refs_2_), channel_id=1, source_target_pairs={{0,8},{1,9},{2,10},{3,11},{4,12},{5,13},{6,14},{7,15},{8,0},{9,1},... | collective-permute-start | bytes 811016 | tf_op jit(solution)/shard_map/ppermute | solution.py:51
  15.9 20.4 %collective-permute-start.6 = (bf16[528,256]{1,0:T(8,128)(2,1)S(1)}, bf16[528,256]{1,0:T(8,128)(2,1)S(1)}, u32[]{:S(2)}, u32[]{:S(2)}) collective-permute-start(bf16[528,256]{1,0:T(8,128)(2,1)S(1)} %collective-permute-done.5.refs_4_), channel_id=1, source_target_pairs={{0,17},{1,16},{2,19},{3,18},{4,21},{5,20},{6,23},{7,22},{8,25},{9,... | collective-permute-start | bytes 811016 | tf_op jit(solution)/shard_map/ppermute | solution.py:51
  18.3 18.0 %collective-permute-start.4 = (bf16[528,256]{1,0:T(8,128)(2,1)S(1)}, bf16[528,256]{1,0:T(8,128)(2,1)S(1)}, u32[]{:S(2)}, u32[]{:S(2)}) collective-permute-start(bf16[528,256]{1,0:T(8,128)(2,1)S(1)} %collective-permute-done.3.refs_3_), channel_id=1, source_target_pairs={{0,2},{1,3},{2,4},{3,5},{4,6},{5,7},{6,0},{7,1},{8,14},{9,15},{10,... | collective-permute-start | bytes 811016 | tf_op jit(solution)/shard_map/ppermute | solution.py:51
  18.7 17.6 %collective-permute-start.2 = (bf16[528,256]{1,0:T(8,128)(2,1)S(1)}, bf16[528,256]{1,0:T(8,128)(2,1)S(1)}, u32[]{:S(2)}, u32[]{:S(2)}) collective-permute-start(bf16[528,256]{1,0:T(8,128)(2,1)S(1)} %collective-permute-done.refs_2_), channel_id=1, source_target_pairs={{0,19},{1,18},{2,21},{3,20},{4,23},{5,22},{6,17},{7,16},{8,31},{9,... | collective-permute-start | bytes 811016 | tf_op jit(solution)/shard_map/ppermute | solution.py:51
  19.7 16.6 %collective-permute-start.1 = (bf16[528,256]{1,0:T(8,128)(2,1)S(1)}, bf16[528,256]{1,0:T(8,128)(2,1)S(1)}, u32[]{:S(2)}, u32[]{:S(2)}) collective-permute-start(bf16[528,256]{1,0:T(8,128)(2,1)S(1)} %collective-permute-done.refs_2_), channel_id=1, source_target_pairs={{0,2},{1,3},{2,4},{3,5},{4,6},{5,7},{6,0},{7,1},{8,14},{9,15},{10,... | collective-permute-start | bytes 811016 | tf_op jit(solution)/shard_map/ppermute | solution.py:51
  20.1 1.2 %copy-start.1 = (bf16[1024,512]{1,0:T(8,128)(2,1)S(1)}, bf16[1024,512]{1,0:T(8,128)(2,1)}, u32[]{:S(2)}) copy-start(bf16[1024,512]{1,0:T(8,128)(2,1)} %queries_ref.5) | copy-start | bytes 3145732
  21.4 0.7 copy-start.3
  36.2 10.4 %copy-start.2 = (bf16[1024,512]{1,0:T(8,128)(2,1)S(1)}, bf16[1024,512]{1,0:T(8,128)(2,1)}, u32[]{:S(2)}) copy-start(bf16[1024,512]{1,0:T(8,128)(2,1)} %queries_ref.5) | copy-start | bytes 3145732
  36.3 10.3 %collective-permute-start.10 = (bf16[528,256]{1,0:T(8,128)(2,1)S(1)}, bf16[528,256]{1,0:T(8,128)(2,1)S(1)}, u32[]{:S(2)}, u32[]{:S(2)}) collective-permute-start(bf16[528,256]{1,0:T(8,128)(2,1)S(1)} %collective-permute-done.1.refs_0_), channel_id=1, source_target_pairs={{0,8},{1,9},{2,10},{3,11},{4,12},{5,13},{6,14},{7,15},{8,0},{9,1},... | collective-permute-start | bytes 811016 | tf_op jit(solution)/shard_map/ppermute | solution.py:51
  37.4 9.3 %collective-permute-start.11 = (bf16[528,256]{1,0:T(8,128)(2,1)S(1)}, bf16[528,256]{1,0:T(8,128)(2,1)S(1)}, u32[]{:S(2)}, u32[]{:S(2)}) collective-permute-start(bf16[528,256]{1,0:T(8,128)(2,1)S(1)} %collective-permute-done.2.refs_1_), channel_id=1, source_target_pairs={{0,8},{1,9},{2,10},{3,11},{4,12},{5,13},{6,14},{7,15},{8,0},{9,1},... | collective-permute-start | bytes 811016 | tf_op jit(solution)/shard_map/ppermute | solution.py:51
  37.5 9.2 %collective-permute-start.12 = (bf16[528,256]{1,0:T(8,128)(2,1)S(1)}, bf16[528,256]{1,0:T(8,128)(2,1)S(1)}, u32[]{:S(2)}, u32[]{:S(2)}) collective-permute-start(bf16[528,256]{1,0:T(8,128)(2,1)S(1)} %collective-permute-done.4.refs_2_), channel_id=1, source_target_pairs={{0,8},{1,9},{2,10},{3,11},{4,12},{5,13},{6,14},{7,15},{8,0},{9,1},... | collective-permute-start | bytes 811016 | tf_op jit(solution)/shard_map/ppermute | solution.py:51
  37.9 8.8 %collective-permute-start.13 = (bf16[528,256]{1,0:T(8,128)(2,1)S(1)}, bf16[528,256]{1,0:T(8,128)(2,1)S(1)}, u32[]{:S(2)}, u32[]{:S(2)}) collective-permute-start(bf16[528,256]{1,0:T(8,128)(2,1)S(1)} %collective-permute-done.6.refs_3_), channel_id=1, source_target_pairs={{0,8},{1,9},{2,10},{3,11},{4,12},{5,13},{6,14},{7,15},{8,0},{9,1},... | collective-permute-start | bytes 811016 | tf_op jit(solution)/shard_map/ppermute | solution.py:51

commit v3 on v2

--- a/solution.py
+++ b/solution.py
@@ -18,6 +18,7 @@
 SCALE = 320.0 * LOG2E
 MARGIN = 58.0
 PANEL = 32
+SPREAD = 16
 REDO = 128
 F32 = jnp.float32
 BF16 = jnp.bfloat16
@@ -304,9 +305,67 @@
     return jnp.broadcast_to(block[at : at + 1, :], block.shape)
 
 
+def three_way(value):
+    high = value.astype(BF16)
+    rest = value - high.astype(F32)
+    middle = rest.astype(BF16)
+    return high, middle, (rest - middle.astype(F32)).astype(BF16)
+
+
+def exact_outer(a, b):
+    a0, a1, a2 = three_way(a)
+    b0, b1, b2 = three_way(b)
+    left = jnp.concatenate([a2, a0, a1, a1, a0, a0], axis=0)
+    right = jnp.concatenate([b0, b2, b1, b0, b1, b0], axis=0)
+    return lax.dot_general(left, right, (((0,), (0,)), ((), ())), preferred_element_type=F32)
+
+
+def eliminate(tiles, square, sub):
+    groups, pivots = len(tiles), []
+    at_tile, at_lane = divmod(square, 128)
+    for base in range(0, PANEL, SPREAD):
+        columns = [
+            {
+                g: jnp.broadcast_to(tiles[g][at_tile][:, lane : lane + 1], (8, 128))
+                for g in range((base + k) // 8, groups)
+            }
+            for k, lane in enumerate(range(at_lane + base, at_lane + base + SPREAD))
+        ]
+        for k in range(0, SPREAD, 2):
+            own, at = divmod(base + k, 8)
+            first, second = columns[k], columns[k + 1]
+            a, b = repeat_row(first[own], at), repeat_row(first[own], at + 1)
+            c = repeat_row(second[own], at + 1)
+            inverse0 = 1.0 / a
+            inverse1 = a * (1.0 / (a * c - b * b))
+            pivots += [inverse0, inverse1]
+            below = range(own, groups)
+            first_low = {g: jnp.where(sub > at, first[g], 0.0) if g == own else first[g] for g in below}
+            multiple0 = {g: first_low[g] * inverse0 for g in below}
+            second_low = {g: second[g] - multiple0[g] * b for g in below}
+            second_low[own] = jnp.where(sub > at + 1, second_low[own], 0.0)
+            multiple1 = {g: second_low[g] * inverse1 for g in below}
+            for m in range(k + 2, SPREAD):
+                group, row = divmod(base + m, 8)
+                factor0 = repeat_row(first[group], row)
+                factor1 = repeat_row(second_low[group], row)
+                for g in columns[m]:
+                    if m < k + 4:
+                        step = (second_low[g] * factor1) * inverse1
+                        columns[m][g] = (columns[m][g] - multiple0[g] * factor0) - step
+                    else:
+                        step = multiple0[g] * factor0 + multiple1[g] * factor1
+                        columns[m][g] = columns[m][g] - step
+            for t in range(len(tiles[own])):
+                for multiple, row in ((multiple0, at), (multiple1, at + 1)):
+                    factor = repeat_row(tiles[own][t], row)
+                    for g in below:
+                        tiles[g][t] = tiles[g][t] - multiple[g] * factor
+    return pivots
+
+
 def inverse_factor(schur, size):
-    groups = PANEL // 8
-    panels = size // PANEL
+    groups, panels = PANEL // 8, size // PANEL
     sub = lax.broadcasted_iota(jnp.int32, (8, 128), 0)
     eye = (
         lax.broadcasted_iota(jnp.int32, (PANEL, PANEL), 0)
@@ -331,34 +390,7 @@
             + [right[8 * g : 8 * g + 8, 128 * k : 128 * k + 128] for k in range(nr)]
             for g in range(groups)
         ]
-        square = left[:, start - lane0 : start - lane0 + PANEL]
-        spread = [
-            [
-                jnp.broadcast_to(square[8 * g : 8 * g + 8, k : k + 1], (8, 128))
-                if g >= k // 8
-                else None
-                for g in range(groups)
-            ]
-            for k in range(PANEL)
-        ]
-        inverses = []
-        for k in range(PANEL):
-            own, at = divmod(k, 8)
-            inv = 1.0 / repeat_row(spread[k][own], at)
-            inverses.append(inv)
-            column = [
-                spread[k][g] if g > own else jnp.where(sub > at, spread[k][g], 0.0) if g == own else None
-                for g in range(groups)
-            ]
-            for m in range(k + 1, PANEL):
-                factor = repeat_row(spread[k][m // 8], m % 8)
-                for g in range(m // 8, groups):
-                    spread[m][g] = spread[m][g] - (column[g] * factor) * inv
-            multiple = [None if c is None else c * inv for c in column]
-            for k2 in range(nl + nr):
-                row = repeat_row(tiles[own][k2], at)
-                for g in range(own, groups):
-                    tiles[g][k2] = tiles[g][k2] - multiple[g] * row
+        inverses = eliminate(tiles, start - lane0, sub)
         scale = []
         for g in range(groups):
             column = inverses[8 * g]
@@ -389,13 +421,7 @@
         for low, high in ((t + 1, t + 2), (t + 2, panels)):
             if low >= high:
                 continue
-            update = lax.dot_general(
-                scaled[:, low * PANEL - lane0 : high * PANEL - lane0],
-                upper,
-                (((0,), (0,)), ((), ())),
-                precision=EXACT,
-                preferred_element_type=F32,
-            )
+            update = exact_outer(scaled[:, low * PANEL - lane0 : high * PANEL - lane0], upper)
             for i in range(low, high):
                 part = update[(i - low) * PANEL : (i - low + 1) * PANEL]
                 kept = [schur[i][:, :lane0]] if lane0 else []

time: 112 us -> 110 us (0.982)
  Pallas kernels: 43.5 us -> 41.3 us
    pallas_call x1, Pallas kernels: 10.5 us -> 8.28 us  [whiten(): pl.pallas_call(whiten_kernel, in_specs=[VMEM, VMEM], out_specs=VMEM, out_...]
  transfers between devices with their start and end apart: 14 -> 14, of which waited for: 2 -> 2; matrix products, arithmetic and copies ran while one was open for 0% -> 0% of each run, Pallas kernels for 20% -> 21%
where the time goes in v3:
time: 110 us
  blocking collectives  44.7 us (41%)
  Pallas kernels  41.3 us (38%)
  starting transfers between devices  17.2 us (16%)
  local copies, waits for them, and re-layouts  2.98 us (3%)
  waiting for transfers between devices  2.62 us (2%)
    ppermute x14, starting transfers between devices, send(): return lax.ppermute(value, ALL, route(move))  17.2 us
    all_to_all x1, blocking collectives, all_sum(): parts = lax.all_to_all(moments.reshape(plane, rows, TARGETS), PLANE, 0, 0)  15.4 us
    all_to_all x1, blocking collectives, all_sum(): lax.all_to_all(jnp.broadcast_to(part, (line, rows, TARGETS)), 'z', 0, 0)  15.3 us
    pallas_call x1, Pallas kernels, first_part(): pl.pallas_call(first_kernel, in_specs=[VMEM] * (2 + len(pieces)), out_spe...  14.2 us
    all_to_all x1, blocking collectives, all_sum(): lax.all_to_all(jnp.broadcast_to(part, (plane, rows, TARGETS)), PLANE, 0, 0)  14.1 us
    pallas_call x1, Pallas kernels, last_part(): pl.pallas_call(functools.partial(last_kernel, len(pieces)), in_specs=[VME...  9.96 us
    pallas_call x1, Pallas kernels, more_part(): pl.pallas_call(more_kernel, in_specs=[VMEM] * (2 + len(pieces)), out_spec...  8.65 us
    pallas_call x1, Pallas kernels, whiten(): pl.pallas_call(whiten_kernel, in_specs=[VMEM, VMEM], out_specs=VMEM, out_...  8.28 us
  transfers between devices with their start and end apart: 14, of which 2 were waited for; matrix products, arithmetic and copies ran while one was open for 0% of the time, Pallas kernels for 21%

profile of v3, /device:TPU:1, one launch (start us, length us, event | category | flops | bytes accessed | tf_op | source)
XLA Modules:
  0.0 109.8 jit_solution(972446770696817471)
XLA Ops:
  0.0 0.7 convert_add_fusion
  0.7 1.0 copy-done
  1.7 0.2 prepare.1
  2.0 3.6 %collective-permute-start.5 = (bf16[528,256]{1,0:T(8,128)(2,1)S(1)}, bf16[528,256]{1,0:T(8,128)(2,1)S(1)}, u32[]{:S(2)}, u32[]{:S(2)}) collective-permute-start(bf16[528,256]{1,0:T(8,128)(2,1)S(1)} %get-tuple-element.15.refs_1_), channel_id=1, source_target_pairs={{0,2},{1,3},{2,4},{3,5},{4,6},{5,7},{6,0},{7,1},{8,14},{9,15},{10,... | collective-permute-start | bytes 811016 | tf_op jit(solution)/shard_map/ppermute | solution.py:52
  5.6 2.5 %collective-permute-start.3 = (bf16[528,256]{1,0:T(8,128)(2,1)S(1)}, bf16[528,256]{1,0:T(8,128)(2,1)S(1)}, u32[]{:S(2)}, u32[]{:S(2)}) collective-permute-start(bf16[528,256]{1,0:T(8,128)(2,1)S(1)} %get-tuple-element.14.refs_0_), channel_id=1, source_target_pairs={{0,17},{1,16},{2,19},{3,18},{4,21},{5,20},{6,23},{7,22},{8,25},{9,... | collective-permute-start | bytes 811016 | tf_op jit(solution)/shard_map/ppermute | solution.py:52
  8.1 0.5 collective-permute-start
  8.6 0.5 collective-permute-done.5.refs_4_
  9.0 3.9 %collective-permute-start.9 = (bf16[528,256]{1,0:T(8,128)(2,1)S(1)}, bf16[528,256]{1,0:T(8,128)(2,1)S(1)}, u32[]{:S(2)}, u32[]{:S(2)}) collective-permute-start(bf16[528,256]{1,0:T(8,128)(2,1)S(1)} %collective-permute-done.5.refs_4_), channel_id=1, source_target_pairs={{0,8},{1,9},{2,10},{3,11},{4,12},{5,13},{6,14},{7,15},{8,0},{9,1},... | collective-permute-start | bytes 811016 | tf_op jit(solution)/shard_map/ppermute | solution.py:52
  13.0 2.1 %collective-permute-done.3.refs_3_ = bf16[528,256]{1,0:T(8,128)(2,1)S(1)} collective-permute-done((bf16[528,256]{1,0:T(8,128)(2,1)S(1)}, bf16[528,256]{1,0:T(8,128)(2,1)S(1)}, u32[]{:S(2)}, u32[]{:S(2)}) %collective-permute-start.3) | collective-permute-done | bytes 270368 | tf_op jit(solution)/shard_map/ppermute | solution.py:52
  15.1 0.6 collective-permute-start.8
  15.7 0.1 collective-permute-start.7
  15.9 2.4 %collective-permute-start.6 = (bf16[528,256]{1,0:T(8,128)(2,1)S(1)}, bf16[528,256]{1,0:T(8,128)(2,1)S(1)}, u32[]{:S(2)}, u32[]{:S(2)}) collective-permute-start(bf16[528,256]{1,0:T(8,128)(2,1)S(1)} %collective-permute-done.5.refs_4_), channel_id=1, source_target_pairs={{0,17},{1,16},{2,19},{3,18},{4,21},{5,20},{6,23},{7,22},{8,25},{9,... | collective-permute-start | bytes 811016 | tf_op jit(solution)/shard_map/ppermute | solution.py:52
  18.3 0.4 collective-permute-start.4
  18.7 1.0 collective-permute-start.2
  19.7 0.0 collective-permute-done.8.refs_6_
  19.7 0.5 collective-permute-start.1
  20.1 1.2 %copy-done.1 = bf16[1024,512]{1,0:T(8,128)(2,1)S(1)} copy-done((bf16[1024,512]{1,0:T(8,128)(2,1)S(1)}, bf16[1024,512]{1,0:T(8,128)(2,1)}, u32[]{:S(2)}) %copy-start.1) | copy-done | bytes 1048600
  21.4 0.7 copy-done.3
  22.1 14.2 %first_part.1.state_in = f32[1024,384]{1,0:T(8,128)S(1)} custom-call(bf16[1024,512]{1,0:T(8,128)(2,1)S(1)} %copy-done.1, f32[8,128]{1,0:T(8,128)S(1)} %bitcast.8, bf16[528,256]{1,0:T(8,128)(2,1)S(1)} %get-tuple-element.14.refs_0_, bf16[528,256]{1,0:T(8,128)(2,1)S(1)} %get-tuple-element.15.refs_1_, bf16[528,256]{1,0:T(8,128)(2,1)S(1)} %collective-permute-done.refs_2_, ...), custom_call_target="tpu_custom_call" | custom-call | flops 9663676416 | bytes 4259840 | tf_op jit(solution)/shard_map/first_part/pallas_call | solution.py:265
  36.2 0.0 copy-start.2
  36.3 0.0 collective-permute-done.6.refs_3_
  36.3 0.0 collective-permute-done.2.refs_1_
  36.3 1.1 collective-permute-start.10
  37.4 0.1 collective-permute-start.11
  37.5 0.4 collective-permute-start.12
  37.9 0.1 collective-permute-start.13
  38.0 8.7 %more_part.1.state_in = f32[1024,384]{1,0:T(8,128)S(1)} custom-call(bf16[1024,512]{1,0:T(8,128)(2,1)S(1)} %copy-done.1, f32[1024,384]{1,0:T(8,128)S(1)} %first_part.1.state_in, bf16[528,256]{1,0:T(8,128)(2,1)S(1)} %collective-permute-done.1.refs_0_, bf16[528,256]{1,0:T(8,128)(2,1)S(1)} %collective-permute-done.2.refs_1_, ...), custom_call_target="tpu_custom_call", output_to_operand_aliasing={{}: (1, {})} | custom-call | flops 4831838208 | bytes 3178496 | tf_op jit(solution)/shard_map/more_part/pallas_call | solution.py:278
  46.7 10.0 %last_part.1 = (f32[1024,384]{1,0:T(8,128)S(1)}, f32[256,256]{1,0:T(8,128)S(1)}) custom-call(bf16[1024,512]{1,0:T(8,128)(2,1)S(1)} %copy-done.2, f32[1024,384]{1,0:T(8,128)S(1)} %more_part.1.state_in, bf16[528,256]{1,0:T(8,128)(2,1)S(1)} %collective-permute-done.10.refs_0_, ...), custom_call_target="tpu_custom_call", output_to_operand_aliasing={{0}: (1, {})} | custom-call | flops 4831838208 | bytes 3178496 | tf_op jit(solution)/shard_map/last_part/pallas_call | solution.py:292
  56.6 15.4 %all_to_all.15 = f32[32,8,256]{2,1,0:T(8,128)S(1)} all-to-all(f32[32,8,256]{2,1,0:T(8,128)S(1)} %bitcast.6), channel_id=1, replica_groups=mesh['z'=8,'x_lo'=2,'core'=2,'y'=4,'x_hi'=2] {'x_lo','core','y','x_hi'}, dimensions={0} | all-to-all | bytes 524288 | tf_op jit(solution)/shard_map/all_to_all | solution.py:476
  72.1 15.3 %all_to_all.16 = f32[8,8,256]{2,1,0:T(8,128)S(1)} all-to-all(f32[8,8,256]{2,1,0:T(8,128)S(1)} %broadcast_in_dim.7), channel_id=1, replica_groups=mesh['z'=8,'x_lo'=2,'core'=2,'y'=4,'x_hi'=2] {'z'}, dimensions={0} | all-to-all | bytes 131072 | tf_op jit(solution)/shard_map/all_to_all | solution.py:478
  87.4 14.1 %all_to_all.17 = f32[32,8,256]{2,1,0:T(8,128)S(1)} all-to-all(f32[32,8,256]{2,1,0:T(8,128)S(1)} %broadcast_in_dim.8), channel_id=1, replica_groups=mesh['z'=8,'x_lo'=2,'core'=2,'y'=4,'x_hi'=2] {'x_lo','core','y','x_hi'}, dimensions={0} | all-to-all | bytes 524288 | tf_op jit(solution)/shard_map/all_to_all | solution.py:480
  101.5 8.3 %whiten.1 = f32[1024,256]{1,0:T(8,128)} custom-call(f32[256,256]{1,0:T(8,128)S(1)} %bitcast.5, f32[1024,384]{1,0:T(8,128)S(1)} %get-tuple-element.22.state_ref), custom_call_target="tpu_custom_call" | custom-call | tf_op jit(solution)/shard_map/whiten/pallas_call | solution.py:463
  (17 shorter events, 0.1 us)
Async XLA Ops:
  0.7 1.0 copy-start
  2.0 7.0 %collective-permute-start.5 = (bf16[528,256]{1,0:T(8,128)(2,1)S(1)}, bf16[528,256]{1,0:T(8,128)(2,1)S(1)}, u32[]{:S(2)}, u32[]{:S(2)}) collective-permute-start(bf16[528,256]{1,0:T(8,128)(2,1)S(1)} %get-tuple-element.15.refs_1_), channel_id=1, source_target_pairs={{0,2},{1,3},{2,4},{3,5},{4,6},{5,7},{6,0},{7,1},{8,14},{9,15},{10,... | collective-permute-start | bytes 811016 | tf_op jit(solution)/shard_map/ppermute | solution.py:52
  5.6 9.5 %collective-permute-start.3 = (bf16[528,256]{1,0:T(8,128)(2,1)S(1)}, bf16[528,256]{1,0:T(8,128)(2,1)S(1)}, u32[]{:S(2)}, u32[]{:S(2)}) collective-permute-start(bf16[528,256]{1,0:T(8,128)(2,1)S(1)} %get-tuple-element.14.refs_0_), channel_id=1, source_target_pairs={{0,17},{1,16},{2,19},{3,18},{4,21},{5,20},{6,23},{7,22},{8,25},{9,... | collective-permute-start | bytes 811016 | tf_op jit(solution)/shard_map/ppermute | solution.py:52
  8.1 7.6 %collective-permute-start = (bf16[528,256]{1,0:T(8,128)(2,1)S(1)}, bf16[528,256]{1,0:T(8,128)(2,1)S(1)}, u32[]{:S(2)}, u32[]{:S(2)}) collective-permute-start(bf16[528,256]{1,0:T(8,128)(2,1)S(1)} %get-tuple-element.14.refs_0_), channel_id=1, source_target_pairs={{0,2},{1,3},{2,4},{3,5},{4,6},{5,7},{6,0},{7,1},{8,14},{9,15},{10,... | collective-permute-start | bytes 811016 | tf_op jit(solution)/shard_map/ppermute | solution.py:52
  9.0 9.7 %collective-permute-start.9 = (bf16[528,256]{1,0:T(8,128)(2,1)S(1)}, bf16[528,256]{1,0:T(8,128)(2,1)S(1)}, u32[]{:S(2)}, u32[]{:S(2)}) collective-permute-start(bf16[528,256]{1,0:T(8,128)(2,1)S(1)} %collective-permute-done.5.refs_4_), channel_id=1, source_target_pairs={{0,8},{1,9},{2,10},{3,11},{4,12},{5,13},{6,14},{7,15},{8,0},{9,1},... | collective-permute-start | bytes 811016 | tf_op jit(solution)/shard_map/ppermute | solution.py:52
  15.1 4.6 %collective-permute-start.8 = (bf16[528,256]{1,0:T(8,128)(2,1)S(1)}, bf16[528,256]{1,0:T(8,128)(2,1)S(1)}, u32[]{:S(2)}, u32[]{:S(2)}) collective-permute-start(bf16[528,256]{1,0:T(8,128)(2,1)S(1)} %collective-permute-done.3.refs_3_), channel_id=1, source_target_pairs={{0,8},{1,9},{2,10},{3,11},{4,12},{5,13},{6,14},{7,15},{8,0},{9,1},... | collective-permute-start | bytes 811016 | tf_op jit(solution)/shard_map/ppermute | solution.py:52
  15.7 4.4 %collective-permute-start.7 = (bf16[528,256]{1,0:T(8,128)(2,1)S(1)}, bf16[528,256]{1,0:T(8,128)(2,1)S(1)}, u32[]{:S(2)}, u32[]{:S(2)}) collective-permute-start(bf16[528,256]{1,0:T(8,128)(2,1)S(1)} %collective-permute-done.refs_2_), channel_id=1, source_target_pairs={{0,8},{1,9},{2,10},{3,11},{4,12},{5,13},{6,14},{7,15},{8,0},{9,1},... | collective-permute-start | bytes 811016 | tf_op jit(solution)/shard_map/ppermute | solution.py:52
  15.9 20.4 %collective-permute-start.6 = (bf16[528,256]{1,0:T(8,128)(2,1)S(1)}, bf16[528,256]{1,0:T(8,128)(2,1)S(1)}, u32[]{:S(2)}, u32[]{:S(2)}) collective-permute-start(bf16[528,256]{1,0:T(8,128)(2,1)S(1)} %collective-permute-done.5.refs_4_), channel_id=1, source_target_pairs={{0,17},{1,16},{2,19},{3,18},{4,21},{5,20},{6,23},{7,22},{8,25},{9,... | collective-permute-start | bytes 811016 | tf_op jit(solution)/shard_map/ppermute | solution.py:52
  18.3 18.0 %collective-permute-start.4 = (bf16[528,256]{1,0:T(8,128)(2,1)S(1)}, bf16[528,256]{1,0:T(8,128)(2,1)S(1)}, u32[]{:S(2)}, u32[]{:S(2)}) collective-permute-start(bf16[528,256]{1,0:T(8,128)(2,1)S(1)} %collective-permute-done.3.refs_3_), channel_id=1, source_target_pairs={{0,2},{1,3},{2,4},{3,5},{4,6},{5,7},{6,0},{7,1},{8,14},{9,15},{10,... | collective-permute-start | bytes 811016 | tf_op jit(solution)/shard_map/ppermute | solution.py:52
  18.7 17.6 %collective-permute-start.2 = (bf16[528,256]{1,0:T(8,128)(2,1)S(1)}, bf16[528,256]{1,0:T(8,128)(2,1)S(1)}, u32[]{:S(2)}, u32[]{:S(2)}) collective-permute-start(bf16[528,256]{1,0:T(8,128)(2,1)S(1)} %collective-permute-done.refs_2_), channel_id=1, source_target_pairs={{0,19},{1,18},{2,21},{3,20},{4,23},{5,22},{6,17},{7,16},{8,31},{9,... | collective-permute-start | bytes 811016 | tf_op jit(solution)/shard_map/ppermute | solution.py:52
  19.7 16.6 %collective-permute-start.1 = (bf16[528,256]{1,0:T(8,128)(2,1)S(1)}, bf16[528,256]{1,0:T(8,128)(2,1)S(1)}, u32[]{:S(2)}, u32[]{:S(2)}) collective-permute-start(bf16[528,256]{1,0:T(8,128)(2,1)S(1)} %collective-permute-done.refs_2_), channel_id=1, source_target_pairs={{0,2},{1,3},{2,4},{3,5},{4,6},{5,7},{6,0},{7,1},{8,14},{9,15},{10,... | collective-permute-start | bytes 811016 | tf_op jit(solution)/shard_map/ppermute | solution.py:52
  20.1 1.2 %copy-start.1 = (bf16[1024,512]{1,0:T(8,128)(2,1)S(1)}, bf16[1024,512]{1,0:T(8,128)(2,1)}, u32[]{:S(2)}) copy-start(bf16[1024,512]{1,0:T(8,128)(2,1)} %queries_ref.5) | copy-start | bytes 3145732
  21.4 0.7 copy-start.3
  36.2 10.4 %copy-start.2 = (bf16[1024,512]{1,0:T(8,128)(2,1)S(1)}, bf16[1024,512]{1,0:T(8,128)(2,1)}, u32[]{:S(2)}) copy-start(bf16[1024,512]{1,0:T(8,128)(2,1)} %queries_ref.5) | copy-start | bytes 3145732
  36.3 10.3 %collective-permute-start.10 = (bf16[528,256]{1,0:T(8,128)(2,1)S(1)}, bf16[528,256]{1,0:T(8,128)(2,1)S(1)}, u32[]{:S(2)}, u32[]{:S(2)}) collective-permute-start(bf16[528,256]{1,0:T(8,128)(2,1)S(1)} %collective-permute-done.1.refs_0_), channel_id=1, source_target_pairs={{0,8},{1,9},{2,10},{3,11},{4,12},{5,13},{6,14},{7,15},{8,0},{9,1},... | collective-permute-start | bytes 811016 | tf_op jit(solution)/shard_map/ppermute | solution.py:52
  37.4 9.3 %collective-permute-start.11 = (bf16[528,256]{1,0:T(8,128)(2,1)S(1)}, bf16[528,256]{1,0:T(8,128)(2,1)S(1)}, u32[]{:S(2)}, u32[]{:S(2)}) collective-permute-start(bf16[528,256]{1,0:T(8,128)(2,1)S(1)} %collective-permute-done.2.refs_1_), channel_id=1, source_target_pairs={{0,8},{1,9},{2,10},{3,11},{4,12},{5,13},{6,14},{7,15},{8,0},{9,1},... | collective-permute-start | bytes 811016 | tf_op jit(solution)/shard_map/ppermute | solution.py:52
  37.5 9.2 %collective-permute-start.12 = (bf16[528,256]{1,0:T(8,128)(2,1)S(1)}, bf16[528,256]{1,0:T(8,128)(2,1)S(1)}, u32[]{:S(2)}, u32[]{:S(2)}) collective-permute-start(bf16[528,256]{1,0:T(8,128)(2,1)S(1)} %collective-permute-done.4.refs_2_), channel_id=1, source_target_pairs={{0,8},{1,9},{2,10},{3,11},{4,12},{5,13},{6,14},{7,15},{8,0},{9,1},... | collective-permute-start | bytes 811016 | tf_op jit(solution)/shard_map/ppermute | solution.py:52
  37.9 8.8 %collective-permute-start.13 = (bf16[528,256]{1,0:T(8,128)(2,1)S(1)}, bf16[528,256]{1,0:T(8,128)(2,1)S(1)}, u32[]{:S(2)}, u32[]{:S(2)}) collective-permute-start(bf16[528,256]{1,0:T(8,128)(2,1)S(1)} %collective-permute-done.6.refs_3_), channel_id=1, source_target_pairs={{0,8},{1,9},{2,10},{3,11},{4,12},{5,13},{6,14},{7,15},{8,0},{9,1},... | collective-permute-start | bytes 811016 | tf_op jit(solution)/shard_map/ppermute | solution.py:52

commit v4 on v3

--- a/solution.py
+++ b/solution.py
@@ -130,8 +130,8 @@
 def add_piece(scores, top, piece_ref, num, den):
     expo = jnp.exp2(scores - top).astype(BF16)
     rounded = expo.astype(F32)
-    for k in range(expo.shape[1] // 128):
-        den = den + rounded[:, k * 128 : (k + 1) * 128]
+    tiles = [rounded[:, k : k + 128] for k in range(0, rounded.shape[1], 128)]
+    den = den + functools.reduce(jnp.add, tiles)
     num = num + lax.dot_general(
         expo,
         piece_values(piece_ref),
@@ -163,7 +163,7 @@
     return jnp.zeros((rows, TARGETS), F32), jnp.zeros((rows, 128), F32)
 
 
-def add_pieces(queries_ref, state_in, state_ref, pieces, weight=None):
+def add_pieces(queries_ref, state_in, state_ref, pieces, weight=None, finish=False):
     queries = queries_ref[...]
     query_norm = squared_norm(queries)
     if state_in is None:
@@ -178,9 +178,14 @@
         num, den = add_piece(scores, top, piece_ref, num, den)
     fits = jnp.max(den) <= 1.0
 
+    def store(rows, num, den, top, weight):
+        if finish:
+            num = num * (1.0 / jnp.sum(den, axis=1, keepdims=True))
+        state_ref[rows, :] = pack(num, den, top, weight)
+
     @pl.when(fits)
     def _():
-        state_ref[...] = pack(num, den, top, weight)
+        store(slice(None), num, den, top, weight)
 
     @pl.when(jnp.logical_not(fits))
     def _():
@@ -208,7 +213,7 @@
             for piece_ref in pieces:
                 scores = piece_scores(queries, query_norm, piece_ref)
                 num, den = add_piece(scores, top, piece_ref, num, den)
-            state_ref[here, :] = pack(num, den, top, weight)
+            store(here, num, den, top, weight)
 
 
 def first_kernel(queries_ref, weight_ref, *refs):
@@ -228,10 +233,8 @@
 
 def last_kernel(count, queries_ref, state_in, *refs):
     state_ref, moments_ref = refs[count:]
-    add_pieces(queries_ref, state_in, state_ref, refs[:count])
-    num, den, _, weight = unpack(state_ref[...])
-    profile = num * (1.0 / jnp.sum(den, axis=1, keepdims=True))
-    state_ref[:, :TARGETS] = profile
+    add_pieces(queries_ref, state_in, state_ref, refs[:count], finish=True)
+    profile, _, _, weight = unpack(state_ref[...])
     weight_total = jnp.sum(weight, axis=0, keepdims=True)
     first = jnp.sum(profile * weight, axis=0, keepdims=True)
     mean = first / weight_total

time: 110 us -> 110 us (level)
  no operation moved by 1% of the time
where the time goes in v4:
time: 110 us
  blocking collectives  44.7 us (41%)
  Pallas kernels  41.1 us (37%)
  starting transfers between devices  17.2 us (16%)
  local copies, waits for them, and re-layouts  2.98 us (3%)
  waiting for transfers between devices  2.62 us (2%)
    ppermute x14, starting transfers between devices, send(): return lax.ppermute(value, ALL, route(move))  17.2 us
    all_to_all x1, blocking collectives, all_sum(): parts = lax.all_to_all(moments.reshape(plane, rows, TARGETS), PLANE, 0, 0)  15.4 us
    all_to_all x1, blocking collectives, all_sum(): lax.all_to_all(jnp.broadcast_to(part, (line, rows, TARGETS)), 'z', 0, 0)  15.3 us
    pallas_call x1, Pallas kernels, first_part(): pl.pallas_call(first_kernel, in_specs=[VMEM] * (2 + len(pieces)), out_spe...  14.2 us
    all_to_all x1, blocking collectives, all_sum(): lax.all_to_all(jnp.broadcast_to(part, (plane, rows, TARGETS)), PLANE, 0, 0)  14.1 us
    pallas_call x1, Pallas kernels, last_part(): pl.pallas_call(functools.partial(last_kernel, len(pieces)), in_specs=[VME...  9.8 us
    pallas_call x1, Pallas kernels, more_part(): pl.pallas_call(more_kernel, in_specs=[VMEM] * (2 + len(pieces)), out_spec...  8.6 us
    pallas_call x1, Pallas kernels, whiten(): pl.pallas_call(whiten_kernel, in_specs=[VMEM, VMEM], out_specs=VMEM, out_...  8.28 us
  transfers between devices with their start and end apart: 14, of which 2 were waited for; matrix products, arithmetic and copies ran while one was open for 0% of the time, Pallas kernels for 21%

profile of v4, /device:TPU:1, one launch (start us, length us, event | category | flops | bytes accessed | tf_op | source)
XLA Modules:
  0.0 109.6 jit_solution(3379504655358548511)
XLA Ops:
  0.0 0.7 convert_add_fusion
  0.7 1.0 copy-done
  1.7 0.2 prepare.1
  2.0 3.6 %collective-permute-start.5 = (bf16[528,256]{1,0:T(8,128)(2,1)S(1)}, bf16[528,256]{1,0:T(8,128)(2,1)S(1)}, u32[]{:S(2)}, u32[]{:S(2)}) collective-permute-start(bf16[528,256]{1,0:T(8,128)(2,1)S(1)} %get-tuple-element.15.refs_1_), channel_id=1, source_target_pairs={{0,2},{1,3},{2,4},{3,5},{4,6},{5,7},{6,0},{7,1},{8,14},{9,15},{10,... | collective-permute-start | bytes 811016 | tf_op jit(solution)/shard_map/ppermute | solution.py:52
  5.6 2.5 %collective-permute-start.3 = (bf16[528,256]{1,0:T(8,128)(2,1)S(1)}, bf16[528,256]{1,0:T(8,128)(2,1)S(1)}, u32[]{:S(2)}, u32[]{:S(2)}) collective-permute-start(bf16[528,256]{1,0:T(8,128)(2,1)S(1)} %get-tuple-element.14.refs_0_), channel_id=1, source_target_pairs={{0,17},{1,16},{2,19},{3,18},{4,21},{5,20},{6,23},{7,22},{8,25},{9,... | collective-permute-start | bytes 811016 | tf_op jit(solution)/shard_map/ppermute | solution.py:52
  8.1 0.5 collective-permute-start
  8.6 0.5 collective-permute-done.5.refs_4_
  9.0 3.9 %collective-permute-start.9 = (bf16[528,256]{1,0:T(8,128)(2,1)S(1)}, bf16[528,256]{1,0:T(8,128)(2,1)S(1)}, u32[]{:S(2)}, u32[]{:S(2)}) collective-permute-start(bf16[528,256]{1,0:T(8,128)(2,1)S(1)} %collective-permute-done.5.refs_4_), channel_id=1, source_target_pairs={{0,8},{1,9},{2,10},{3,11},{4,12},{5,13},{6,14},{7,15},{8,0},{9,1},... | collective-permute-start | bytes 811016 | tf_op jit(solution)/shard_map/ppermute | solution.py:52
  13.0 2.1 %collective-permute-done.3.refs_3_ = bf16[528,256]{1,0:T(8,128)(2,1)S(1)} collective-permute-done((bf16[528,256]{1,0:T(8,128)(2,1)S(1)}, bf16[528,256]{1,0:T(8,128)(2,1)S(1)}, u32[]{:S(2)}, u32[]{:S(2)}) %collective-permute-start.3) | collective-permute-done | bytes 270368 | tf_op jit(solution)/shard_map/ppermute | solution.py:52
  15.1 0.6 collective-permute-start.8
  15.7 0.1 collective-permute-start.7
  15.9 2.4 %collective-permute-start.6 = (bf16[528,256]{1,0:T(8,128)(2,1)S(1)}, bf16[528,256]{1,0:T(8,128)(2,1)S(1)}, u32[]{:S(2)}, u32[]{:S(2)}) collective-permute-start(bf16[528,256]{1,0:T(8,128)(2,1)S(1)} %collective-permute-done.5.refs_4_), channel_id=1, source_target_pairs={{0,17},{1,16},{2,19},{3,18},{4,21},{5,20},{6,23},{7,22},{8,25},{9,... | collective-permute-start | bytes 811016 | tf_op jit(solution)/shard_map/ppermute | solution.py:52
  18.3 0.4 collective-permute-start.4
  18.7 1.0 collective-permute-start.2
  19.7 0.0 collective-permute-done.8.refs_6_
  19.7 0.5 collective-permute-start.1
  20.1 1.2 %copy-done.1 = bf16[1024,512]{1,0:T(8,128)(2,1)S(1)} copy-done((bf16[1024,512]{1,0:T(8,128)(2,1)S(1)}, bf16[1024,512]{1,0:T(8,128)(2,1)}, u32[]{:S(2)}) %copy-start.1) | copy-done | bytes 1048600
  21.4 0.7 copy-done.3
  22.1 14.2 %first_part.1.state_in = f32[1024,384]{1,0:T(8,128)S(1)} custom-call(bf16[1024,512]{1,0:T(8,128)(2,1)S(1)} %copy-done.1, f32[8,128]{1,0:T(8,128)S(1)} %bitcast.8, bf16[528,256]{1,0:T(8,128)(2,1)S(1)} %get-tuple-element.14.refs_0_, bf16[528,256]{1,0:T(8,128)(2,1)S(1)} %get-tuple-element.15.refs_1_, bf16[528,256]{1,0:T(8,128)(2,1)S(1)} %collective-permute-done.refs_2_, ...), custom_call_target="tpu_custom_call" | custom-call | flops 9663676416 | bytes 4259840 | tf_op jit(solution)/shard_map/first_part/pallas_call | solution.py:268
  36.3 0.0 copy-start.2
  36.3 0.0 collective-permute-done.4.refs_2_
  36.3 1.1 collective-permute-start.10
  37.4 0.1 collective-permute-start.11
  37.5 0.4 collective-permute-start.12
  37.9 0.1 collective-permute-start.13
  38.0 8.6 %more_part.1.state_in = f32[1024,384]{1,0:T(8,128)S(1)} custom-call(bf16[1024,512]{1,0:T(8,128)(2,1)S(1)} %copy-done.1, f32[1024,384]{1,0:T(8,128)S(1)} %first_part.1.state_in, bf16[528,256]{1,0:T(8,128)(2,1)S(1)} %collective-permute-done.1.refs_0_, bf16[528,256]{1,0:T(8,128)(2,1)S(1)} %collective-permute-done.2.refs_1_, ...), custom_call_target="tpu_custom_call", output_to_operand_aliasing={{}: (1, {})} | custom-call | flops 4831838208 | bytes 3178496 | tf_op jit(solution)/shard_map/more_part/pallas_call | solution.py:281
  46.6 0.0 collective-permute-done.11.refs_1_
  46.7 9.8 %last_part.1 = (f32[1024,384]{1,0:T(8,128)S(1)}, f32[256,256]{1,0:T(8,128)S(1)}) custom-call(bf16[1024,512]{1,0:T(8,128)(2,1)S(1)} %copy-done.2, f32[1024,384]{1,0:T(8,128)S(1)} %more_part.1.state_in, bf16[528,256]{1,0:T(8,128)(2,1)S(1)} %collective-permute-done.10.refs_0_, ...), custom_call_target="tpu_custom_call", output_to_operand_aliasing={{0}: (1, {})} | custom-call | flops 4831838208 | bytes 3178496 | tf_op jit(solution)/shard_map/last_part/pallas_call | solution.py:295
  56.5 15.4 %all_to_all.15 = f32[32,8,256]{2,1,0:T(8,128)S(1)} all-to-all(f32[32,8,256]{2,1,0:T(8,128)S(1)} %bitcast.6), channel_id=1, replica_groups=mesh['z'=8,'x_lo'=2,'core'=2,'y'=4,'x_hi'=2] {'x_lo','core','y','x_hi'}, dimensions={0} | all-to-all | bytes 524288 | tf_op jit(solution)/shard_map/all_to_all | solution.py:479
  71.9 15.3 %all_to_all.16 = f32[8,8,256]{2,1,0:T(8,128)S(1)} all-to-all(f32[8,8,256]{2,1,0:T(8,128)S(1)} %broadcast_in_dim.7), channel_id=1, replica_groups=mesh['z'=8,'x_lo'=2,'core'=2,'y'=4,'x_hi'=2] {'z'}, dimensions={0} | all-to-all | bytes 131072 | tf_op jit(solution)/shard_map/all_to_all | solution.py:481
  87.2 14.1 %all_to_all.17 = f32[32,8,256]{2,1,0:T(8,128)S(1)} all-to-all(f32[32,8,256]{2,1,0:T(8,128)S(1)} %broadcast_in_dim.8), channel_id=1, replica_groups=mesh['z'=8,'x_lo'=2,'core'=2,'y'=4,'x_hi'=2] {'x_lo','core','y','x_hi'}, dimensions={0} | all-to-all | bytes 524288 | tf_op jit(solution)/shard_map/all_to_all | solution.py:483
  101.3 8.3 %whiten.1 = f32[1024,256]{1,0:T(8,128)} custom-call(f32[256,256]{1,0:T(8,128)S(1)} %bitcast.5, f32[1024,384]{1,0:T(8,128)S(1)} %get-tuple-element.22.state_ref), custom_call_target="tpu_custom_call" | custom-call | tf_op jit(solution)/shard_map/whiten/pallas_call | solution.py:466
  (17 shorter events, 0.1 us)
Async XLA Ops:
  0.7 1.0 copy-start
  2.0 7.0 %collective-permute-start.5 = (bf16[528,256]{1,0:T(8,128)(2,1)S(1)}, bf16[528,256]{1,0:T(8,128)(2,1)S(1)}, u32[]{:S(2)}, u32[]{:S(2)}) collective-permute-start(bf16[528,256]{1,0:T(8,128)(2,1)S(1)} %get-tuple-element.15.refs_1_), channel_id=1, source_target_pairs={{0,2},{1,3},{2,4},{3,5},{4,6},{5,7},{6,0},{7,1},{8,14},{9,15},{10,... | collective-permute-start | bytes 811016 | tf_op jit(solution)/shard_map/ppermute | solution.py:52
  5.6 9.5 %collective-permute-start.3 = (bf16[528,256]{1,0:T(8,128)(2,1)S(1)}, bf16[528,256]{1,0:T(8,128)(2,1)S(1)}, u32[]{:S(2)}, u32[]{:S(2)}) collective-permute-start(bf16[528,256]{1,0:T(8,128)(2,1)S(1)} %get-tuple-element.14.refs_0_), channel_id=1, source_target_pairs={{0,17},{1,16},{2,19},{3,18},{4,21},{5,20},{6,23},{7,22},{8,25},{9,... | collective-permute-start | bytes 811016 | tf_op jit(solution)/shard_map/ppermute | solution.py:52
  8.1 7.6 %collective-permute-start = (bf16[528,256]{1,0:T(8,128)(2,1)S(1)}, bf16[528,256]{1,0:T(8,128)(2,1)S(1)}, u32[]{:S(2)}, u32[]{:S(2)}) collective-permute-start(bf16[528,256]{1,0:T(8,128)(2,1)S(1)} %get-tuple-element.14.refs_0_), channel_id=1, source_target_pairs={{0,2},{1,3},{2,4},{3,5},{4,6},{5,7},{6,0},{7,1},{8,14},{9,15},{10,... | collective-permute-start | bytes 811016 | tf_op jit(solution)/shard_map/ppermute | solution.py:52
  9.0 9.7 %collective-permute-start.9 = (bf16[528,256]{1,0:T(8,128)(2,1)S(1)}, bf16[528,256]{1,0:T(8,128)(2,1)S(1)}, u32[]{:S(2)}, u32[]{:S(2)}) collective-permute-start(bf16[528,256]{1,0:T(8,128)(2,1)S(1)} %collective-permute-done.5.refs_4_), channel_id=1, source_target_pairs={{0,8},{1,9},{2,10},{3,11},{4,12},{5,13},{6,14},{7,15},{8,0},{9,1},... | collective-permute-start | bytes 811016 | tf_op jit(solution)/shard_map/ppermute | solution.py:52
  15.1 4.6 %collective-permute-start.8 = (bf16[528,256]{1,0:T(8,128)(2,1)S(1)}, bf16[528,256]{1,0:T(8,128)(2,1)S(1)}, u32[]{:S(2)}, u32[]{:S(2)}) collective-permute-start(bf16[528,256]{1,0:T(8,128)(2,1)S(1)} %collective-permute-done.3.refs_3_), channel_id=1, source_target_pairs={{0,8},{1,9},{2,10},{3,11},{4,12},{5,13},{6,14},{7,15},{8,0},{9,1},... | collective-permute-start | bytes 811016 | tf_op jit(solution)/shard_map/ppermute | solution.py:52
  15.7 4.4 %collective-permute-start.7 = (bf16[528,256]{1,0:T(8,128)(2,1)S(1)}, bf16[528,256]{1,0:T(8,128)(2,1)S(1)}, u32[]{:S(2)}, u32[]{:S(2)}) collective-permute-start(bf16[528,256]{1,0:T(8,128)(2,1)S(1)} %collective-permute-done.refs_2_), channel_id=1, source_target_pairs={{0,8},{1,9},{2,10},{3,11},{4,12},{5,13},{6,14},{7,15},{8,0},{9,1},... | collective-permute-start | bytes 811016 | tf_op jit(solution)/shard_map/ppermute | solution.py:52
  15.9 20.4 %collective-permute-start.6 = (bf16[528,256]{1,0:T(8,128)(2,1)S(1)}, bf16[528,256]{1,0:T(8,128)(2,1)S(1)}, u32[]{:S(2)}, u32[]{:S(2)}) collective-permute-start(bf16[528,256]{1,0:T(8,128)(2,1)S(1)} %collective-permute-done.5.refs_4_), channel_id=1, source_target_pairs={{0,17},{1,16},{2,19},{3,18},{4,21},{5,20},{6,23},{7,22},{8,25},{9,... | collective-permute-start | bytes 811016 | tf_op jit(solution)/shard_map/ppermute | solution.py:52
  18.3 18.0 %collective-permute-start.4 = (bf16[528,256]{1,0:T(8,128)(2,1)S(1)}, bf16[528,256]{1,0:T(8,128)(2,1)S(1)}, u32[]{:S(2)}, u32[]{:S(2)}) collective-permute-start(bf16[528,256]{1,0:T(8,128)(2,1)S(1)} %collective-permute-done.3.refs_3_), channel_id=1, source_target_pairs={{0,2},{1,3},{2,4},{3,5},{4,6},{5,7},{6,0},{7,1},{8,14},{9,15},{10,... | collective-permute-start | bytes 811016 | tf_op jit(solution)/shard_map/ppermute | solution.py:52
  18.7 17.6 %collective-permute-start.2 = (bf16[528,256]{1,0:T(8,128)(2,1)S(1)}, bf16[528,256]{1,0:T(8,128)(2,1)S(1)}, u32[]{:S(2)}, u32[]{:S(2)}) collective-permute-start(bf16[528,256]{1,0:T(8,128)(2,1)S(1)} %collective-permute-done.refs_2_), channel_id=1, source_target_pairs={{0,19},{1,18},{2,21},{3,20},{4,23},{5,22},{6,17},{7,16},{8,31},{9,... | collective-permute-start | bytes 811016 | tf_op jit(solution)/shard_map/ppermute | solution.py:52
  19.7 16.6 %collective-permute-start.1 = (bf16[528,256]{1,0:T(8,128)(2,1)S(1)}, bf16[528,256]{1,0:T(8,128)(2,1)S(1)}, u32[]{:S(2)}, u32[]{:S(2)}) collective-permute-start(bf16[528,256]{1,0:T(8,128)(2,1)S(1)} %collective-permute-done.refs_2_), channel_id=1, source_target_pairs={{0,2},{1,3},{2,4},{3,5},{4,6},{5,7},{6,0},{7,1},{8,14},{9,15},{10,... | collective-permute-start | bytes 811016 | tf_op jit(solution)/shard_map/ppermute | solution.py:52
  20.1 1.2 %copy-start.1 = (bf16[1024,512]{1,0:T(8,128)(2,1)S(1)}, bf16[1024,512]{1,0:T(8,128)(2,1)}, u32[]{:S(2)}) copy-start(bf16[1024,512]{1,0:T(8,128)(2,1)} %queries_ref.5) | copy-start | bytes 3145732
  21.4 0.7 copy-start.3
  36.3 10.4 %copy-start.2 = (bf16[1024,512]{1,0:T(8,128)(2,1)S(1)}, bf16[1024,512]{1,0:T(8,128)(2,1)}, u32[]{:S(2)}) copy-start(bf16[1024,512]{1,0:T(8,128)(2,1)} %queries_ref.5) | copy-start | bytes 3145732
  36.3 10.3 %collective-permute-start.10 = (bf16[528,256]{1,0:T(8,128)(2,1)S(1)}, bf16[528,256]{1,0:T(8,128)(2,1)S(1)}, u32[]{:S(2)}, u32[]{:S(2)}) collective-permute-start(bf16[528,256]{1,0:T(8,128)(2,1)S(1)} %collective-permute-done.1.refs_0_), channel_id=1, source_target_pairs={{0,8},{1,9},{2,10},{3,11},{4,12},{5,13},{6,14},{7,15},{8,0},{9,1},... | collective-permute-start | bytes 811016 | tf_op jit(solution)/shard_map/ppermute | solution.py:52
  37.4 9.2 %collective-permute-start.11 = (bf16[528,256]{1,0:T(8,128)(2,1)S(1)}, bf16[528,256]{1,0:T(8,128)(2,1)S(1)}, u32[]{:S(2)}, u32[]{:S(2)}) collective-permute-start(bf16[528,256]{1,0:T(8,128)(2,1)S(1)} %collective-permute-done.2.refs_1_), channel_id=1, source_target_pairs={{0,8},{1,9},{2,10},{3,11},{4,12},{5,13},{6,14},{7,15},{8,0},{9,1},... | collective-permute-start | bytes 811016 | tf_op jit(solution)/shard_map/ppermute | solution.py:52
  37.5 9.1 %collective-permute-start.12 = (bf16[528,256]{1,0:T(8,128)(2,1)S(1)}, bf16[528,256]{1,0:T(8,128)(2,1)S(1)}, u32[]{:S(2)}, u32[]{:S(2)}) collective-permute-start(bf16[528,256]{1,0:T(8,128)(2,1)S(1)} %collective-permute-done.4.refs_2_), channel_id=1, source_target_pairs={{0,8},{1,9},{2,10},{3,11},{4,12},{5,13},{6,14},{7,15},{8,0},{9,1},... | collective-permute-start | bytes 811016 | tf_op jit(solution)/shard_map/ppermute | solution.py:52
  37.9 8.7 %collective-permute-start.13 = (bf16[528,256]{1,0:T(8,128)(2,1)S(1)}, bf16[528,256]{1,0:T(8,128)(2,1)S(1)}, u32[]{:S(2)}, u32[]{:S(2)}) collective-permute-start(bf16[528,256]{1,0:T(8,128)(2,1)S(1)} %collective-permute-done.6.refs_3_), channel_id=1, source_target_pairs={{0,8},{1,9},{2,10},{3,11},{4,12},{5,13},{6,14},{7,15},{8,0},{9,1},... | collective-permute-start | bytes 811016 | tf_op jit(solution)/shard_map/ppermute | solution.py:52

commit v5 on v3

--- a/solution.py
+++ b/solution.py
@@ -22,7 +22,6 @@
 REDO = 128
 F32 = jnp.float32
 BF16 = jnp.bfloat16
-EXACT = lax.Precision.HIGHEST
 VMEM = pl.BlockSpec(memory_space=pltpu.VMEM)
 
 
@@ -240,9 +239,7 @@
     high, low = split(spread)
     cross = lax.dot_general(high, low, outer, preferred_element_type=F32)
     moments = lax.dot_general(high, high, outer, preferred_element_type=F32) + (cross + cross.T)
-    moments = moments + lax.dot_general(
-        mean, first, outer, precision=EXACT, preferred_element_type=F32
-    )
+    moments = moments + jnp.broadcast_to(mean, (TARGETS, TARGETS)).T * first
     row = lax.broadcasted_iota(jnp.int32, (TARGETS, TARGETS), 0)
     column = lax.broadcasted_iota(jnp.int32, (TARGETS, TARGETS), 1)
     moments = jnp.where((row == 0) & (column > 0), first, moments)
@@ -440,9 +437,7 @@
     share = 1.0 / total[1:2, 3:4]
     first = jnp.where(column[0:1] == 0, total[1:2, 2:3], total[0:1, :])
     mean = first * share
-    outer = lax.dot_general(
-        mean, mean, (((0,), (0,)), ((), ())), precision=EXACT, preferred_element_type=F32
-    )
+    outer = jnp.broadcast_to(mean, (TARGETS, TARGETS)).T * mean
     lower = jnp.where(column <= row, total, 0.0)
     strict = jnp.where(column < row, total, 0.0)
     covariance = (lower + strict.T) * share - outer

time: 110 us -> 109 us (level)
  no operation moved by 1% of the time
where the time goes in v5:
time: 109 us
  blocking collectives  44.7 us (41%)
  Pallas kernels  40.7 us (37%)
  starting transfers between devices  17.2 us (16%)
  local copies, waits for them, and re-layouts  2.98 us (3%)
  waiting for transfers between devices  2.62 us (2%)
    ppermute x14, starting transfers between devices, send(): return lax.ppermute(value, ALL, route(move))  17.2 us
    all_to_all x1, blocking collectives, all_sum(): parts = lax.all_to_all(moments.reshape(plane, rows, TARGETS), PLANE, 0, 0)  15.4 us
    all_to_all x1, blocking collectives, all_sum(): lax.all_to_all(jnp.broadcast_to(part, (line, rows, TARGETS)), 'z', 0, 0)  15.3 us
    pallas_call x1, Pallas kernels, first_part(): pl.pallas_call(first_kernel, in_specs=[VMEM] * (2 + len(pieces)), out_spe...  14.2 us
    all_to_all x1, blocking collectives, all_sum(): lax.all_to_all(jnp.broadcast_to(part, (plane, rows, TARGETS)), PLANE, 0, 0)  14.1 us
    pallas_call x1, Pallas kernels, last_part(): pl.pallas_call(functools.partial(last_kernel, len(pieces)), in_specs=[VME...  9.83 us
    pallas_call x1, Pallas kernels, more_part(): pl.pallas_call(more_kernel, in_specs=[VMEM] * (2 + len(pieces)), out_spec...  8.65 us
    pallas_call x1, Pallas kernels, whiten(): pl.pallas_call(whiten_kernel, in_specs=[VMEM, VMEM], out_specs=VMEM, out_...  7.82 us
  transfers between devices with their start and end apart: 14, of which 2 were waited for; matrix products, arithmetic and copies ran while one was open for 0% of the time, Pallas kernels for 21%

profile of v5, /device:TPU:1, one launch (start us, length us, event | category | flops | bytes accessed | tf_op | source)
XLA Modules:
  0.0 109.2 jit_solution(16069831332980381010)
XLA Ops:
  0.0 0.7 convert_add_fusion
  0.7 1.0 copy-done
  1.7 0.2 prepare.1
  2.0 3.6 %collective-permute-start.5 = (bf16[528,256]{1,0:T(8,128)(2,1)S(1)}, bf16[528,256]{1,0:T(8,128)(2,1)S(1)}, u32[]{:S(2)}, u32[]{:S(2)}) collective-permute-start(bf16[528,256]{1,0:T(8,128)(2,1)S(1)} %get-tuple-element.15.refs_1_), channel_id=1, source_target_pairs={{0,2},{1,3},{2,4},{3,5},{4,6},{5,7},{6,0},{7,1},{8,14},{9,15},{10,... | collective-permute-start | bytes 811016 | tf_op jit(solution)/shard_map/ppermute | solution.py:51
  5.6 2.5 %collective-permute-start.3 = (bf16[528,256]{1,0:T(8,128)(2,1)S(1)}, bf16[528,256]{1,0:T(8,128)(2,1)S(1)}, u32[]{:S(2)}, u32[]{:S(2)}) collective-permute-start(bf16[528,256]{1,0:T(8,128)(2,1)S(1)} %get-tuple-element.14.refs_0_), channel_id=1, source_target_pairs={{0,17},{1,16},{2,19},{3,18},{4,21},{5,20},{6,23},{7,22},{8,25},{9,... | collective-permute-start | bytes 811016 | tf_op jit(solution)/shard_map/ppermute | solution.py:51
  8.1 0.5 collective-permute-start
  8.6 0.5 collective-permute-done.5.refs_4_
  9.0 3.9 %collective-permute-start.9 = (bf16[528,256]{1,0:T(8,128)(2,1)S(1)}, bf16[528,256]{1,0:T(8,128)(2,1)S(1)}, u32[]{:S(2)}, u32[]{:S(2)}) collective-permute-start(bf16[528,256]{1,0:T(8,128)(2,1)S(1)} %collective-permute-done.5.refs_4_), channel_id=1, source_target_pairs={{0,8},{1,9},{2,10},{3,11},{4,12},{5,13},{6,14},{7,15},{8,0},{9,1},... | collective-permute-start | bytes 811016 | tf_op jit(solution)/shard_map/ppermute | solution.py:51
  13.0 2.1 %collective-permute-done.3.refs_3_ = bf16[528,256]{1,0:T(8,128)(2,1)S(1)} collective-permute-done((bf16[528,256]{1,0:T(8,128)(2,1)S(1)}, bf16[528,256]{1,0:T(8,128)(2,1)S(1)}, u32[]{:S(2)}, u32[]{:S(2)}) %collective-permute-start.3) | collective-permute-done | bytes 270368 | tf_op jit(solution)/shard_map/ppermute | solution.py:51
  15.1 0.6 collective-permute-start.8
  15.7 0.1 collective-permute-start.7
  15.9 2.4 %collective-permute-start.6 = (bf16[528,256]{1,0:T(8,128)(2,1)S(1)}, bf16[528,256]{1,0:T(8,128)(2,1)S(1)}, u32[]{:S(2)}, u32[]{:S(2)}) collective-permute-start(bf16[528,256]{1,0:T(8,128)(2,1)S(1)} %collective-permute-done.5.refs_4_), channel_id=1, source_target_pairs={{0,17},{1,16},{2,19},{3,18},{4,21},{5,20},{6,23},{7,22},{8,25},{9,... | collective-permute-start | bytes 811016 | tf_op jit(solution)/shard_map/ppermute | solution.py:51
  18.3 0.4 collective-permute-start.4
  18.7 1.0 collective-permute-start.2
  19.7 0.0 collective-permute-done.8.refs_6_
  19.7 0.5 collective-permute-start.1
  20.1 1.2 %copy-done.1 = bf16[1024,512]{1,0:T(8,128)(2,1)S(1)} copy-done((bf16[1024,512]{1,0:T(8,128)(2,1)S(1)}, bf16[1024,512]{1,0:T(8,128)(2,1)}, u32[]{:S(2)}) %copy-start.1) | copy-done | bytes 1048600
  21.4 0.7 copy-done.3
  22.1 14.2 %first_part.1.state_in = f32[1024,384]{1,0:T(8,128)S(1)} custom-call(bf16[1024,512]{1,0:T(8,128)(2,1)S(1)} %copy-done.1, f32[8,128]{1,0:T(8,128)S(1)} %bitcast.8, bf16[528,256]{1,0:T(8,128)(2,1)S(1)} %get-tuple-element.14.refs_0_, bf16[528,256]{1,0:T(8,128)(2,1)S(1)} %get-tuple-element.15.refs_1_, bf16[528,256]{1,0:T(8,128)(2,1)S(1)} %collective-permute-done.refs_2_, ...), custom_call_target="tpu_custom_call" | custom-call | flops 9663676416 | bytes 4259840 | tf_op jit(solution)/shard_map/first_part/pallas_call | solution.py:262
  36.2 0.0 copy-start.2
  36.3 0.0 collective-permute-done.6.refs_3_
  36.3 0.0 collective-permute-done.2.refs_1_
  36.3 1.1 collective-permute-start.10
  37.4 0.1 collective-permute-start.11
  37.5 0.4 collective-permute-start.12
  37.9 0.1 collective-permute-start.13
  38.0 8.7 %more_part.1.state_in = f32[1024,384]{1,0:T(8,128)S(1)} custom-call(bf16[1024,512]{1,0:T(8,128)(2,1)S(1)} %copy-done.1, f32[1024,384]{1,0:T(8,128)S(1)} %first_part.1.state_in, bf16[528,256]{1,0:T(8,128)(2,1)S(1)} %collective-permute-done.1.refs_0_, bf16[528,256]{1,0:T(8,128)(2,1)S(1)} %collective-permute-done.2.refs_1_, ...), custom_call_target="tpu_custom_call", output_to_operand_aliasing={{}: (1, {})} | custom-call | flops 4831838208 | bytes 3178496 | tf_op jit(solution)/shard_map/more_part/pallas_call | solution.py:275
  46.7 9.8 %last_part.1 = (f32[1024,384]{1,0:T(8,128)S(1)}, f32[256,256]{1,0:T(8,128)S(1)}) custom-call(bf16[1024,512]{1,0:T(8,128)(2,1)S(1)} %copy-done.2, f32[1024,384]{1,0:T(8,128)S(1)} %more_part.1.state_in, bf16[528,256]{1,0:T(8,128)(2,1)S(1)} %collective-permute-done.10.refs_0_, ...), custom_call_target="tpu_custom_call", output_to_operand_aliasing={{0}: (1, {})} | custom-call | flops 4831838208 | bytes 3178496 | tf_op jit(solution)/shard_map/last_part/pallas_call | solution.py:289
  56.5 15.4 %all_to_all.15 = f32[32,8,256]{2,1,0:T(8,128)S(1)} all-to-all(f32[32,8,256]{2,1,0:T(8,128)S(1)} %bitcast.6), channel_id=1, replica_groups=mesh['z'=8,'x_lo'=2,'core'=2,'y'=4,'x_hi'=2] {'x_lo','core','y','x_hi'}, dimensions={0} | all-to-all | bytes 524288 | tf_op jit(solution)/shard_map/all_to_all | solution.py:471
  72.0 15.3 %all_to_all.16 = f32[8,8,256]{2,1,0:T(8,128)S(1)} all-to-all(f32[8,8,256]{2,1,0:T(8,128)S(1)} %broadcast_in_dim.7), channel_id=1, replica_groups=mesh['z'=8,'x_lo'=2,'core'=2,'y'=4,'x_hi'=2] {'z'}, dimensions={0} | all-to-all | bytes 131072 | tf_op jit(solution)/shard_map/all_to_all | solution.py:473
  87.3 14.1 %all_to_all.17 = f32[32,8,256]{2,1,0:T(8,128)S(1)} all-to-all(f32[32,8,256]{2,1,0:T(8,128)S(1)} %broadcast_in_dim.8), channel_id=1, replica_groups=mesh['z'=8,'x_lo'=2,'core'=2,'y'=4,'x_hi'=2] {'x_lo','core','y','x_hi'}, dimensions={0} | all-to-all | bytes 524288 | tf_op jit(solution)/shard_map/all_to_all | solution.py:475
  101.3 7.8 %whiten.1 = f32[1024,256]{1,0:T(8,128)} custom-call(f32[256,256]{1,0:T(8,128)S(1)} %bitcast.5, f32[1024,384]{1,0:T(8,128)S(1)} %get-tuple-element.22.state_ref), custom_call_target="tpu_custom_call" | custom-call | tf_op jit(solution)/shard_map/whiten/pallas_call | solution.py:458
  (17 shorter events, 0.1 us)
Async XLA Ops:
  0.7 1.0 copy-start
  2.0 7.0 %collective-permute-start.5 = (bf16[528,256]{1,0:T(8,128)(2,1)S(1)}, bf16[528,256]{1,0:T(8,128)(2,1)S(1)}, u32[]{:S(2)}, u32[]{:S(2)}) collective-permute-start(bf16[528,256]{1,0:T(8,128)(2,1)S(1)} %get-tuple-element.15.refs_1_), channel_id=1, source_target_pairs={{0,2},{1,3},{2,4},{3,5},{4,6},{5,7},{6,0},{7,1},{8,14},{9,15},{10,... | collective-permute-start | bytes 811016 | tf_op jit(solution)/shard_map/ppermute | solution.py:51
  5.6 9.5 %collective-permute-start.3 = (bf16[528,256]{1,0:T(8,128)(2,1)S(1)}, bf16[528,256]{1,0:T(8,128)(2,1)S(1)}, u32[]{:S(2)}, u32[]{:S(2)}) collective-permute-start(bf16[528,256]{1,0:T(8,128)(2,1)S(1)} %get-tuple-element.14.refs_0_), channel_id=1, source_target_pairs={{0,17},{1,16},{2,19},{3,18},{4,21},{5,20},{6,23},{7,22},{8,25},{9,... | collective-permute-start | bytes 811016 | tf_op jit(solution)/shard_map/ppermute | solution.py:51
  8.1 7.6 %collective-permute-start = (bf16[528,256]{1,0:T(8,128)(2,1)S(1)}, bf16[528,256]{1,0:T(8,128)(2,1)S(1)}, u32[]{:S(2)}, u32[]{:S(2)}) collective-permute-start(bf16[528,256]{1,0:T(8,128)(2,1)S(1)} %get-tuple-element.14.refs_0_), channel_id=1, source_target_pairs={{0,2},{1,3},{2,4},{3,5},{4,6},{5,7},{6,0},{7,1},{8,14},{9,15},{10,... | collective-permute-start | bytes 811016 | tf_op jit(solution)/shard_map/ppermute | solution.py:51
  9.0 9.7 %collective-permute-start.9 = (bf16[528,256]{1,0:T(8,128)(2,1)S(1)}, bf16[528,256]{1,0:T(8,128)(2,1)S(1)}, u32[]{:S(2)}, u32[]{:S(2)}) collective-permute-start(bf16[528,256]{1,0:T(8,128)(2,1)S(1)} %collective-permute-done.5.refs_4_), channel_id=1, source_target_pairs={{0,8},{1,9},{2,10},{3,11},{4,12},{5,13},{6,14},{7,15},{8,0},{9,1},... | collective-permute-start | bytes 811016 | tf_op jit(solution)/shard_map/ppermute | solution.py:51
  15.1 4.6 %collective-permute-start.8 = (bf16[528,256]{1,0:T(8,128)(2,1)S(1)}, bf16[528,256]{1,0:T(8,128)(2,1)S(1)}, u32[]{:S(2)}, u32[]{:S(2)}) collective-permute-start(bf16[528,256]{1,0:T(8,128)(2,1)S(1)} %collective-permute-done.3.refs_3_), channel_id=1, source_target_pairs={{0,8},{1,9},{2,10},{3,11},{4,12},{5,13},{6,14},{7,15},{8,0},{9,1},... | collective-permute-start | bytes 811016 | tf_op jit(solution)/shard_map/ppermute | solution.py:51
  15.7 4.4 %collective-permute-start.7 = (bf16[528,256]{1,0:T(8,128)(2,1)S(1)}, bf16[528,256]{1,0:T(8,128)(2,1)S(1)}, u32[]{:S(2)}, u32[]{:S(2)}) collective-permute-start(bf16[528,256]{1,0:T(8,128)(2,1)S(1)} %collective-permute-done.refs_2_), channel_id=1, source_target_pairs={{0,8},{1,9},{2,10},{3,11},{4,12},{5,13},{6,14},{7,15},{8,0},{9,1},... | collective-permute-start | bytes 811016 | tf_op jit(solution)/shard_map/ppermute | solution.py:51
  15.9 20.4 %collective-permute-start.6 = (bf16[528,256]{1,0:T(8,128)(2,1)S(1)}, bf16[528,256]{1,0:T(8,128)(2,1)S(1)}, u32[]{:S(2)}, u32[]{:S(2)}) collective-permute-start(bf16[528,256]{1,0:T(8,128)(2,1)S(1)} %collective-permute-done.5.refs_4_), channel_id=1, source_target_pairs={{0,17},{1,16},{2,19},{3,18},{4,21},{5,20},{6,23},{7,22},{8,25},{9,... | collective-permute-start | bytes 811016 | tf_op jit(solution)/shard_map/ppermute | solution.py:51
  18.3 18.0 %collective-permute-start.4 = (bf16[528,256]{1,0:T(8,128)(2,1)S(1)}, bf16[528,256]{1,0:T(8,128)(2,1)S(1)}, u32[]{:S(2)}, u32[]{:S(2)}) collective-permute-start(bf16[528,256]{1,0:T(8,128)(2,1)S(1)} %collective-permute-done.3.refs_3_), channel_id=1, source_target_pairs={{0,2},{1,3},{2,4},{3,5},{4,6},{5,7},{6,0},{7,1},{8,14},{9,15},{10,... | collective-permute-start | bytes 811016 | tf_op jit(solution)/shard_map/ppermute | solution.py:51
  18.7 17.6 %collective-permute-start.2 = (bf16[528,256]{1,0:T(8,128)(2,1)S(1)}, bf16[528,256]{1,0:T(8,128)(2,1)S(1)}, u32[]{:S(2)}, u32[]{:S(2)}) collective-permute-start(bf16[528,256]{1,0:T(8,128)(2,1)S(1)} %collective-permute-done.refs_2_), channel_id=1, source_target_pairs={{0,19},{1,18},{2,21},{3,20},{4,23},{5,22},{6,17},{7,16},{8,31},{9,... | collective-permute-start | bytes 811016 | tf_op jit(solution)/shard_map/ppermute | solution.py:51
  19.7 16.6 %collective-permute-start.1 = (bf16[528,256]{1,0:T(8,128)(2,1)S(1)}, bf16[528,256]{1,0:T(8,128)(2,1)S(1)}, u32[]{:S(2)}, u32[]{:S(2)}) collective-permute-start(bf16[528,256]{1,0:T(8,128)(2,1)S(1)} %collective-permute-done.refs_2_), channel_id=1, source_target_pairs={{0,2},{1,3},{2,4},{3,5},{4,6},{5,7},{6,0},{7,1},{8,14},{9,15},{10,... | collective-permute-start | bytes 811016 | tf_op jit(solution)/shard_map/ppermute | solution.py:51
  20.1 1.2 %copy-start.1 = (bf16[1024,512]{1,0:T(8,128)(2,1)S(1)}, bf16[1024,512]{1,0:T(8,128)(2,1)}, u32[]{:S(2)}) copy-start(bf16[1024,512]{1,0:T(8,128)(2,1)} %queries_ref.5) | copy-start | bytes 3145732
  21.4 0.7 copy-start.3
  36.2 10.4 %copy-start.2 = (bf16[1024,512]{1,0:T(8,128)(2,1)S(1)}, bf16[1024,512]{1,0:T(8,128)(2,1)}, u32[]{:S(2)}) copy-start(bf16[1024,512]{1,0:T(8,128)(2,1)} %queries_ref.5) | copy-start | bytes 3145732
  36.3 10.3 %collective-permute-start.10 = (bf16[528,256]{1,0:T(8,128)(2,1)S(1)}, bf16[528,256]{1,0:T(8,128)(2,1)S(1)}, u32[]{:S(2)}, u32[]{:S(2)}) collective-permute-start(bf16[528,256]{1,0:T(8,128)(2,1)S(1)} %collective-permute-done.1.refs_0_), channel_id=1, source_target_pairs={{0,8},{1,9},{2,10},{3,11},{4,12},{5,13},{6,14},{7,15},{8,0},{9,1},... | collective-permute-start | bytes 811016 | tf_op jit(solution)/shard_map/ppermute | solution.py:51
  37.4 9.3 %collective-permute-start.11 = (bf16[528,256]{1,0:T(8,128)(2,1)S(1)}, bf16[528,256]{1,0:T(8,128)(2,1)S(1)}, u32[]{:S(2)}, u32[]{:S(2)}) collective-permute-start(bf16[528,256]{1,0:T(8,128)(2,1)S(1)} %collective-permute-done.2.refs_1_), channel_id=1, source_target_pairs={{0,8},{1,9},{2,10},{3,11},{4,12},{5,13},{6,14},{7,15},{8,0},{9,1},... | collective-permute-start | bytes 811016 | tf_op jit(solution)/shard_map/ppermute | solution.py:51
  37.5 9.2 %collective-permute-start.12 = (bf16[528,256]{1,0:T(8,128)(2,1)S(1)}, bf16[528,256]{1,0:T(8,128)(2,1)S(1)}, u32[]{:S(2)}, u32[]{:S(2)}) collective-permute-start(bf16[528,256]{1,0:T(8,128)(2,1)S(1)} %collective-permute-done.4.refs_2_), channel_id=1, source_target_pairs={{0,8},{1,9},{2,10},{3,11},{4,12},{5,13},{6,14},{7,15},{8,0},{9,1},... | collective-permute-start | bytes 811016 | tf_op jit(solution)/shard_map/ppermute | solution.py:51
  37.9 8.8 %collective-permute-start.13 = (bf16[528,256]{1,0:T(8,128)(2,1)S(1)}, bf16[528,256]{1,0:T(8,128)(2,1)S(1)}, u32[]{:S(2)}, u32[]{:S(2)}) collective-permute-start(bf16[528,256]{1,0:T(8,128)(2,1)S(1)} %collective-permute-done.6.refs_3_), channel_id=1, source_target_pairs={{0,8},{1,9},{2,10},{3,11},{4,12},{5,13},{6,14},{7,15},{8,0},{9,1},... | collective-permute-start | bytes 811016 | tf_op jit(solution)/shard_map/ppermute | solution.py:51
